TPU v7x, 32 devices: a whole 2x2x4 slice. The times are simulated.
32 devices in a mesh: dp: 4 (over y, x), ctx: 8 (over z, core).
Axes of the slice: x: 2, y: 2, z: 4, core: 2. Of those that a mesh axis runs over, the one named last changes fastest.
Arguments:
- resid: bfloat16 [4096, 2048], P(('dp', 'ctx')), may hold values from -6 to 6
- queries: bfloat16 [4096, 2048], P(('dp', 'ctx')), may hold values from -28 to 28
- keys: bfloat16 [4096, 128], P(('dp', 'ctx')), may hold values from -6 to 6
- values: bfloat16 [4096, 128], P(('dp', 'ctx')), may hold values from -6 to 6
- block_order: int32 [16], replicated, may hold values from 0 to 15, each once
- routes: int32 [4096, 4], P(('dp', 'ctx')), may hold values from 0 to 31, all different within a row; in each aligned block of 128 rows (0 to 127, 128 to 255, ...) at most 20 rows name the same one
- route_weights: float32 [4096, 4], P(('dp', 'ctx')), may hold values from 0.1 to 1
- norm_gain: float32 [2048], replicated, may hold values from 0.5 to 2
- w_gate: bfloat16 [32, 2048, 768], P(('dp', 'ctx')), may hold values from -0.125 to 0.125
- w_up: bfloat16 [32, 2048, 768], P(('dp', 'ctx')), may hold values from -0.125 to 0.125
- w_down: bfloat16 [32, 768, 2048], P(('dp', 'ctx')), may hold values from -0.21875 to 0.21875
- cotangent: bfloat16 [4096, 2048], P(('dp', 'ctx')), may hold values from -6 to 6
Outputs:
- layer_out: bfloat16 [4096, 2048], P(('dp', 'ctx'))
- d_resid: bfloat16 [4096, 2048], P(('dp', 'ctx'))
- d_queries: bfloat16 [4096, 2048], P(('dp', 'ctx'))
- d_keys: bfloat16 [4096, 128], P(('dp', 'ctx'))
- d_values: bfloat16 [4096, 128], P(('dp', 'ctx'))
- d_gain: float32 [2048], replicated
- d_w_gate: bfloat16 [32, 2048, 768], P(('dp', 'ctx'))
- d_w_up: bfloat16 [32, 2048, 768], P(('dp', 'ctx'))
- d_w_down: bfloat16 [32, 768, 2048], P(('dp', 'ctx'))
Inputs may be any that keep to these rules, and one draw needn't show every extreme that they name: `routes`: each row names 4 different experts; the rows of one device name one expert at most 20 times, and that many in some device of every draw. `block_order`: each block number once.
All inputs are finite; a program needn't handle non-finite values.
Results may differ from a plain program's by a relative error of at most 0.023.
Values may be sent and summed in bfloat16 or wider, within the bound.
A program may use at most 128 MiB of HBM per device.

v0:
```python
import math

import jax
import jax.numpy as jnp
from jax import lax
from jax.sharding import PartitionSpec as P

DH = 64


NEG_BIG = -1e30
EPSILON = 1e-06


def contract_rows(left_side, right_side):
    return lax.dot_general(
        left_side, right_side, (((0,), (0,)), ((), ())), preferred_element_type=jnp.float32
    )


def contract_cols(left_side, right_side):
    return lax.dot_general(
        left_side, right_side, (((1,), (1,)), ((), ())), preferred_element_type=jnp.float32
    )


def blockwise(update, running, kv_piece):
    length = kv_piece[0].shape[0]
    block_size = math.gcd(length, 512)

    def advance(number, state_now):
        begin_row = number * block_size
        kv_parts = tuple(
            (lax.dynamic_slice_in_dim(member, begin_row, block_size, 0) for member in kv_piece)
        )
        return update(state_now, kv_parts, begin_row)

    return lax.fori_loop(0, length // block_size, advance, running)


def trade_rows(buffer):
    return lax.all_to_all(buffer, ("dp", "ctx"), split_axis=0, concat_axis=0, tiled=True)


def local(
    resid,
    queries,
    keys,
    values,
    block_order,
    routes,
    route_weights,
    norm_gain,
    w_gate,
    w_up,
    w_down,
    cotangent,
):
    tok_rows, model_width = resid.shape
    kv_heads = keys.shape[1] // DH
    group_size = queries.shape[1] // DH // kv_heads
    block_rows = tok_rows // 2
    ctx_count = lax.axis_size("ctx")
    seq_rows = tok_rows * ctx_count
    scale_factor = DH ** (-0.5)
    local_index = jnp.arange(tok_rows, dtype=jnp.int32)
    query_places = (
        block_order[2 * lax.axis_index("ctx") + local_index // block_rows] * block_rows
        + local_index % block_rows
    )
    query_heads = queries.reshape(tok_rows, kv_heads, group_size, DH)

    def key_places(offset, row_count):
        rows_here = offset + jnp.arange(row_count, dtype=jnp.int32)
        return jnp.take(block_order, rows_here // block_rows) * block_rows + rows_here % block_rows

    def scores_for(key_piece, offset):
        key_heads = key_piece.reshape(-1, kv_heads, DH)
        scores = (
            jnp.einsum("tkgd,pkd->kgtp", query_heads, key_heads, preferred_element_type=jnp.float32)
            * scale_factor
        )
        allowed = query_places[:, None] >= key_places(offset, key_piece.shape[0])[None, :]
        return jnp.where(allowed, scores, NEG_BIG)

    def forward_step(running, kv_piece, offset):
        row_top, totals, accumulated = running
        scores = scores_for(kv_piece[0], offset)
        new_top = jnp.maximum(row_top, jnp.max(scores, axis=-1))
        rescale = jnp.exp(row_top - new_top)
        weights = jnp.exp(scores - new_top[..., None])
        totals = totals * rescale + jnp.sum(weights, axis=-1)
        value_heads = kv_piece[1].reshape(-1, kv_heads, DH)
        gained = jnp.einsum(
            "kgtp,pkd->tkgd",
            weights.astype(jnp.bfloat16),
            value_heads,
            preferred_element_type=jnp.float32,
        )
        accumulated = accumulated * jnp.transpose(rescale, (2, 0, 1))[..., None] + gained
        return (new_top, totals, accumulated)

    head_shape = (kv_heads, group_size, tok_rows)
    start_state = (
        jnp.full(head_shape, NEG_BIG, jnp.float32),
        jnp.zeros(head_shape, jnp.float32),
        jnp.zeros((tok_rows, kv_heads, group_size, DH), jnp.float32),
    )
    row_top, totals, accumulated = blockwise(
        forward_step,
        start_state,
        (
            lax.all_gather(keys, "ctx", axis=0, tiled=True),
            lax.all_gather(values, "ctx", axis=0, tiled=True),
        ),
    )
    attended = (
        (accumulated / jnp.transpose(totals, (2, 0, 1))[..., None])
        .reshape(tok_rows, -1)
        .astype(jnp.bfloat16)
    )
    log_totals = row_top + jnp.log(totals)
    hidden = (resid.astype(jnp.float32) + attended.astype(jnp.float32)).astype(jnp.bfloat16)
    hidden_f = hidden.astype(jnp.float32)
    inv_rms = lax.rsqrt(jnp.mean(hidden_f * hidden_f, axis=-1, keepdims=True) + EPSILON)
    normed = (hidden_f * inv_rms * norm_gain).astype(jnp.bfloat16)
    top_count = routes.shape[1]
    expert_count = lax.axis_size("dp") * ctx_count * w_gate.shape[0]
    capacity = max(2, 5 * tok_rows * top_count // (4 * expert_count))
    flat_routes = routes.reshape(-1)
    onehot = (flat_routes[:, None] == jnp.arange(expert_count, dtype=jnp.int32)[None, :]).astype(
        jnp.int32
    )
    slot_rank = jnp.sum(jnp.cumsum(onehot, axis=0) * onehot, axis=1) - 1
    flat_slots = flat_routes * capacity + slot_rank
    picked = flat_slots[None, :] == jnp.arange(expert_count * capacity, dtype=jnp.int32)[:, None]
    dispatch = jnp.any(picked.reshape(expert_count * capacity, tok_rows, top_count), axis=2).astype(
        jnp.bfloat16
    )
    slot_weights = jnp.dot(
        picked.astype(jnp.float32), route_weights.reshape(-1), precision=lax.Precision.HIGHEST
    )
    buffer_shape = (expert_count, capacity, model_width)
    send_rows = (
        jnp.dot(dispatch, normed, preferred_element_type=jnp.float32)
        .astype(jnp.bfloat16)
        .reshape(buffer_shape)
    )
    grad_out = cotangent.astype(jnp.float32)
    grad_place = jnp.dot(dispatch, cotangent, preferred_element_type=jnp.float32)
    grad_send = (slot_weights[:, None] * grad_place).astype(jnp.bfloat16).reshape(buffer_shape)
    received = trade_rows(send_rows).reshape(-1, model_width)
    gate_w = w_gate[0]
    up_w = w_up[0]
    down_w = w_down[0]
    gate_lin = jnp.dot(received, gate_w, preferred_element_type=jnp.float32)
    up_lin = jnp.dot(received, up_w, preferred_element_type=jnp.float32)
    gate_sig = jax.nn.sigmoid(gate_lin)
    gate_act = gate_lin * gate_sig
    hidden_act = (gate_act * up_lin).astype(jnp.bfloat16)
    produced = jnp.dot(hidden_act, down_w, preferred_element_type=jnp.float32).astype(jnp.bfloat16)
    returned = trade_rows(produced.reshape(buffer_shape)).reshape(-1, model_width)
    grad_recv = trade_rows(grad_send).reshape(-1, model_width)
    grad_act = contract_cols(grad_recv, down_w)
    grad_gate = (grad_act * up_lin * gate_sig * (1.0 + gate_lin * (1.0 - gate_sig))).astype(
        jnp.bfloat16
    )
    grad_up = (grad_act * gate_act).astype(jnp.bfloat16)
    grad_input = (contract_cols(grad_gate, gate_w) + contract_cols(grad_up, up_w)).astype(
        jnp.bfloat16
    )
    d_w_gate = contract_rows(received, grad_gate).astype(jnp.bfloat16)[None]
    d_w_up = contract_rows(received, grad_up).astype(jnp.bfloat16)[None]
    d_w_down = contract_rows(hidden_act, grad_recv).astype(jnp.bfloat16)[None]
    grad_back = trade_rows(grad_input.reshape(buffer_shape)).reshape(-1, model_width)
    gathered = jnp.take(returned, flat_slots, axis=0).reshape(tok_rows, top_count, model_width)
    mixed_moe = jnp.sum(route_weights[..., None] * gathered.astype(jnp.float32), axis=1)
    layer_out = (hidden_f + mixed_moe).astype(jnp.bfloat16)
    grad_normed = jnp.sum(
        jnp.take(grad_back, flat_slots, axis=0)
        .reshape(tok_rows, top_count, model_width)
        .astype(jnp.float32),
        axis=1,
    )
    grad_scaled = grad_normed * norm_gain
    grad_hidden = inv_rms * grad_scaled - hidden_f * inv_rms * inv_rms * inv_rms * jnp.mean(
        grad_scaled * hidden_f, axis=-1, keepdims=True
    )
    d_gain = lax.psum(jnp.sum(grad_normed * hidden_f * inv_rms, axis=0), ("dp", "ctx"))
    d_resid = (grad_out + grad_hidden).astype(jnp.bfloat16)
    grad_heads = d_resid.reshape(tok_rows, kv_heads, group_size, DH)
    out_heads = attended.reshape(tok_rows, kv_heads, group_size, DH)
    row_dots = jnp.transpose(
        jnp.sum(grad_heads.astype(jnp.float32) * out_heads.astype(jnp.float32), axis=-1), (1, 2, 0)
    )

    def backward_step(running, kv_piece, offset):
        grad_query, grad_keys_all, grad_values_all = running
        scores = scores_for(kv_piece[0], offset)
        probabilities = jnp.exp(scores - log_totals[..., None])
        key_heads = kv_piece[0].reshape(-1, kv_heads, DH)
        value_heads = kv_piece[1].reshape(-1, kv_heads, DH)
        grad_value = jnp.einsum(
            "kgtp,tkgd->pkd",
            probabilities.astype(jnp.bfloat16),
            grad_heads,
            preferred_element_type=jnp.float32,
        )
        grad_probs = jnp.einsum(
            "tkgd,pkd->kgtp", grad_heads, value_heads, preferred_element_type=jnp.float32
        )
        grad_scores = (probabilities * (grad_probs - row_dots[..., None]) * scale_factor).astype(
            jnp.bfloat16
        )
        grad_query = grad_query + jnp.einsum(
            "kgtp,pkd->tkgd", grad_scores, key_heads, preferred_element_type=jnp.float32
        )
        grad_key = jnp.einsum(
            "kgtp,tkgd->pkd", grad_scores, query_heads, preferred_element_type=jnp.float32
        )
        rows_now = key_heads.shape[0]
        grad_keys_all = lax.dynamic_update_slice_in_dim(
            grad_keys_all, grad_key.reshape(rows_now, -1), offset, 0
        )
        grad_values_all = lax.dynamic_update_slice_in_dim(
            grad_values_all, grad_value.reshape(rows_now, -1), offset, 0
        )
        return (grad_query, grad_keys_all, grad_values_all)

    back_state = (
        jnp.zeros((tok_rows, kv_heads, group_size, DH), jnp.float32),
        jnp.zeros((seq_rows, kv_heads * DH), jnp.float32),
        jnp.zeros((seq_rows, kv_heads * DH), jnp.float32),
    )
    grad_query, grad_keys_all, grad_values_all = blockwise(
        backward_step,
        back_state,
        (
            lax.all_gather(keys, "ctx", axis=0, tiled=True),
            lax.all_gather(values, "ctx", axis=0, tiled=True),
        ),
    )
    grad_keys_mine, grad_values_mine = (
        lax.psum_scatter(
            grad_keys_all.astype(jnp.bfloat16), "ctx", scatter_dimension=0, tiled=True
        ).astype(jnp.float32),
        lax.psum_scatter(
            grad_values_all.astype(jnp.bfloat16), "ctx", scatter_dimension=0, tiled=True
        ).astype(jnp.float32),
    )
    return (
        layer_out,
        d_resid,
        grad_query.reshape(tok_rows, -1).astype(jnp.bfloat16),
        grad_keys_mine.astype(jnp.bfloat16),
        grad_values_mine.astype(jnp.bfloat16),
        d_gain,
        d_w_gate,
        d_w_up,
        d_w_down,
    )


def solution(mesh):
    return jax.shard_map(
        local,
        mesh=mesh,
        in_specs=(
            P(("dp", "ctx"), None),
            P(("dp", "ctx"), None),
            P(("dp", "ctx"), None),
            P(("dp", "ctx"), None),
            P(),
            P(("dp", "ctx"), None),
            P(("dp", "ctx"), None),
            P(),
            P(("dp", "ctx"), None, None),
            P(("dp", "ctx"), None, None),
            P(("dp", "ctx"), None, None),
            P(("dp", "ctx"), None),
        ),
        out_specs=(
            P(("dp", "ctx"), None),
            P(("dp", "ctx"), None),
            P(("dp", "ctx"), None),
            P(("dp", "ctx"), None),
            P(("dp", "ctx"), None),
            P(),
            P(("dp", "ctx"), None, None),
            P(("dp", "ctx"), None, None),
            P(("dp", "ctx"), None, None),
        ),
        check_vma=False,
    )
```

profile of v0, /device:TPU:0, one launch (start us, length us, event | category | flops | bytes accessed | tf_op | source)
XLA Modules:
  0.0 624.3 jit_solution(15420711139061545350)
XLA Ops:
  13.2 14.8 %all_gather.8 = bf16[1024,128]{0,1:T(8,128)(2,1)S(1)} all-gather(bf16[128,128]{0,1:T(8,128)(2,1)S(1)} %copy.100), channel_id=1, replica_groups=mesh['dp'=4,'ctx'=8] {'ctx'}, dimensions={0}, use_global_device_ids=true | all-gather | bytes 294912 | tf_op jit(solution)/shard_map/all_gather | solution.py:113
  28.9 14.1 %all_gather.9 = bf16[1024,128]{0,1:T(8,128)(2,1)} all-gather(bf16[128,128]{0,1:T(8,128)(2,1)S(1)} %copy.102), channel_id=1, replica_groups=mesh['dp'=4,'ctx'=8] {'ctx'}, dimensions={0}, use_global_device_ids=true | all-gather | bytes 294912 | tf_op jit(solution)/shard_map/all_gather | solution.py:114
  43.0 10.3 %fusion.72 = s32[128]{0:T(128)S(1)} fusion(s32[]{:T(128)} %bitcast.18, s32[]{:T(128)} %bitcast.19, s32[]{:T(128)} %bitcast.20, s32[]{:T(128)} %bitcast.21, s32[]{:T(128)} %bitcast.22, s32[]{:T(128)} %bitcast.24, s32[]{:T(128)} %bitcast.23, s32[]{:T(128)} %bitcast.1, s32[]{:T(128)} %bitcast.3, s32[]{:T(128)} %bitcast.5, s32[]{:T(128)} %bitcast.7, ...), kind=kLoop, calls=%fused_computation.159 | loop fusion | flops 6400 | bytes 580 | tf_op jit(solution)/shard_map/add | solution.py:68
  53.2 56.1 %while.40 = (s32[]{:T(128)}, f32[2,16,128]{2,1,0:T(8,128)S(1)}, f32[2,16,128]{2,1,0:T(8,128)S(1)}, f32[128,2,16,64]{0,3,2,1:T(8,128)}, s32[128]{0:T(128)S(1)}, /...) while((s32[]{:T(128)}, f32[2,16,128]{2,1,0:T(8,128)S(1)}, ...), condition=%wide.region_3.5_spmd.clone, body=%wide.region_0.4_spmd.clone.sunk | while | flops 560846336 | bytes 62657432 | solution.py:38
  55.2 10.3 %fusion.142 = s32[512]{0:T(512)S(1)} fusion(s32[]{:T(128)} %bitcast.340, s32[]{:T(128)} %bitcast.341, s32[]{:T(128)} %bitcast.342, s32[]{:T(128)} %bitcast.343, s32[]{:T(128)} %bitcast.344, s32[]{:T(128)} %bitcast.345, s32[]{:T(128)} %bitcast.346, s32[]{:T(128)} %bitcast.347, s32[]{:T(128)} %bitcast.348, s32[]{:T(128)} %bitcast.349, s32[]{:T(128)} %bitcast.350, ...), kind=kLoop, calls=%fused_computation.24.clone.1 | loop fusion | flops 30208 | bytes 2116 | tf_op jit(solution)/shard_map/while/body/eval_jaxpr/add | solution.py:75
  67.2 5.6 fusion.143
  72.8 6.6 %fusion.147 = f32[128,2,16,64]{0,3,2,1:T(8,128)} fusion(bf16[512,2,64,1]{0,2,3,1:T(8,128)(2,1)} %bitcast.397, f32[2,512,128,16]{2,1,3,0:T(8,128)} %get-tuple-element.936, f32[2,16,128]{2,1,0:T(8,128)S(1)} %get-tuple-element.996, pred[128,512]{0,1:T(8,128)(4,1)S(1)} %broadcast_compare_fusion.4, f32[128,2,16,64]{0,3,2,1:T(8,128)} %get-tuple-element.985, ...), kind=kOutput, calls=%fused_computation.10.clone.1 | convolution fusion | flops 277610496 | bytes 10715137 | tf_op jit(solution)/shard_map/while/body/eval_jaxpr/kgtp,pkd->tkgd/dot_general | solution.py:94
  83.1 10.3 %fusion.142 = s32[512]{0:T(512)S(1)} fusion(s32[]{:T(128)} %bitcast.340, s32[]{:T(128)} %bitcast.341, s32[]{:T(128)} %bitcast.342, s32[]{:T(128)} %bitcast.343, s32[]{:T(128)} %bitcast.344, s32[]{:T(128)} %bitcast.345, s32[]{:T(128)} %bitcast.346, s32[]{:T(128)} %bitcast.347, s32[]{:T(128)} %bitcast.348, s32[]{:T(128)} %bitcast.349, s32[]{:T(128)} %bitcast.350, ...), kind=kLoop, calls=%fused_computation.24.clone.1 | loop fusion | flops 30208 | bytes 2116 | tf_op jit(solution)/shard_map/while/body/eval_jaxpr/add | solution.py:75
  95.1 5.6 fusion.143
  100.7 6.8 %fusion.147 = f32[128,2,16,64]{0,3,2,1:T(8,128)} fusion(bf16[512,2,64,1]{0,2,3,1:T(8,128)(2,1)} %bitcast.397, f32[2,512,128,16]{2,1,3,0:T(8,128)} %get-tuple-element.936, f32[2,16,128]{2,1,0:T(8,128)S(1)} %get-tuple-element.996, pred[128,512]{0,1:T(8,128)(4,1)S(1)} %broadcast_compare_fusion.4, f32[128,2,16,64]{0,3,2,1:T(8,128)} %get-tuple-element.985, ...), kind=kOutput, calls=%fused_computation.10.clone.1 | convolution fusion | flops 277610496 | bytes 10715137 | tf_op jit(solution)/shard_map/while/body/eval_jaxpr/kgtp,pkd->tkgd/dot_general | solution.py:94
  142.6 63.1 %all-to-all-done = bf16[32,20,2048]{2,1,0:T(8,128)(2,1)} async-done(((bf16[32,20,2048]{2,1,0:T(8,128)(2,1)}), bf16[32,20,2048]{2,1,0:T(8,128)(2,1)}, u32[]{:S(2)}, u32[]{:S(2)}) %all-to-all-start) | async-done | bytes 2621472 | tf_op jit(solution)/shard_map/all_to_all | solution.py:42
  214.6 6.3 %fusion.38 = f32[640,768]{1,0:T(8,128)} fusion(bf16[640,2048]{1,0:T(8,128)(2,1)} %reshape.247, bf16[1,2048,768]{2,1,0:T(8,128)(2,1)} %param.29), kind=kOutput, calls=%fused_computation.77 | convolution fusion | flops 2013265920 | bytes 7733248 | tf_op jit(solution)/shard_map/dot_general | solution.py:157
  224.4 57.7 %all-to-all-done.2 = bf16[32,20,2048]{2,1,0:T(8,128)(2,1)} async-done(((bf16[32,20,2048]{2,1,0:T(8,128)(2,1)}), bf16[32,20,2048]{2,1,0:T(8,128)(2,1)}, u32[]{:S(2)}, u32[]{:S(2)}) %all-to-all-start.2) | async-done | bytes 2621472 | tf_op jit(solution)/shard_map/all_to_all | solution.py:42
  287.3 6.9 %multiply_convert_fusion.1 = (bf16[640,768]{1,0:T(8,128)(2,1)S(1)}, bf16[640,768]{1,0:T(8,128)(2,1)S(1)}, bf16[640,768]{1,0:T(8,128)(2,1)}) fusion(f32[640,768]{1,0:T(8,128)} %fusion.42, f32[640,768]{1,0:T(8,128)} %fusion.38, bf16[640,2048]{1,0:T(8,128)(2,1)} %reshape.252, bf16[1,768,2048]{2,1,0:T(8,128)(2,1)S(1)} %copy-done), kind=kOutput, calls=%fused_computation.93 | convolution fusion | flops 2020638720 | bytes 12648448 | tf_op jit(solution)/shard_map/dot_general | solution.py:22
  319.2 62.6 %all-to-all-done.3 = bf16[32,20,2048]{2,1,0:T(8,128)(2,1)} async-done(((bf16[32,20,2048]{2,1,0:T(8,128)(2,1)}), bf16[32,20,2048]{2,1,0:T(8,128)(2,1)}, u32[]{:S(2)}, u32[]{:S(2)}) %all-to-all-start.3) | async-done | bytes 2621472 | tf_op jit(solution)/shard_map/all_to_all | solution.py:42
  392.8 65.2 %all-to-all-done.1 = bf16[32,20,2048]{2,1,0:T(8,128)(2,1)} async-done(((bf16[32,20,2048]{2,1,0:T(8,128)(2,1)}), bf16[32,20,2048]{2,1,0:T(8,128)(2,1)}, u32[]{:S(2)}, u32[]{:S(2)}) %all-to-all-start.1) | async-done | bytes 2621472 | tf_op jit(solution)/shard_map/all_to_all | solution.py:42
  464.9 6.1 select_convert_fusion
  476.2 6.3 %multiply_reduce_fusion = f32[128,2048]{1,0:T(8,128)} fusion(f32[128,4,2048]{2,1,0:T(4,128)} %reshape.257, f32[128,4]{1,0:T(8,128)S(1)} %copy.104), kind=kLoop, calls=%fused_computation.67 | loop fusion | flops 1835008 | bytes 5244928 | tf_op jit(solution)/shard_map/reduce_sum | solution.py:177
  501.2 56.6 %while.41 = (s32[]{:T(128)}, f32[128,2,16,64]{0,3,2,1:T(8,128)S(1)}, bf16[1024,128]{1,0:T(8,128)(2,1)}, bf16[1024,128]{1,0:T(8,128)(2,1)}, bf16[1024,128]{0,1:T(...) while((s32[]{:T(128)}, ...), condition=%wide.region_14.17_spmd.clone, body=%wide.region_13.16_spmd.clone.sunk | while | flops 1365865984 | bytes 94753752 | solution.py:38
  502.1 10.0 %fusion.160 = s32[512]{0:T(512)S(1)} fusion(s32[]{:T(128)} %bitcast.372, s32[]{:T(128)} %bitcast.373, s32[]{:T(128)} %bitcast.374, s32[]{:T(128)} %bitcast.375, s32[]{:T(128)} %bitcast.376, s32[]{:T(128)} %bitcast.377, s32[]{:T(128)} %bitcast.378, s32[]{:T(128)} %bitcast.379, s32[]{:T(128)} %bitcast.380, s32[]{:T(128)} %bitcast.381, s32[]{:T(128)} %bitcast.382, ...), kind=kLoop, calls=%fused_computation.53.clone.1 | loop fusion | flops 30208 | bytes 2116 | tf_op jit(solution)/shard_map/while/body/eval_jaxpr/add | solution.py:75
  530.3 10.0 %fusion.160 = s32[512]{0:T(512)S(1)} fusion(s32[]{:T(128)} %bitcast.372, s32[]{:T(128)} %bitcast.373, s32[]{:T(128)} %bitcast.374, s32[]{:T(128)} %bitcast.375, s32[]{:T(128)} %bitcast.376, s32[]{:T(128)} %bitcast.377, s32[]{:T(128)} %bitcast.378, s32[]{:T(128)} %bitcast.379, s32[]{:T(128)} %bitcast.380, s32[]{:T(128)} %bitcast.381, s32[]{:T(128)} %bitcast.382, ...), kind=kLoop, calls=%fused_computation.53.clone.1 | loop fusion | flops 30208 | bytes 2116 | tf_op jit(solution)/shard_map/while/body/eval_jaxpr/add | solution.py:75
  557.9 6.7 %fusion.44 = bf16[1,2048,768]{2,1,0:T(8,128)(2,1)} fusion(bf16[640,2048]{1,0:T(8,128)(2,1)} %reshape.247, bf16[640,768]{1,0:T(8,128)(2,1)} %copy-done.22), kind=kOutput, calls=%fused_computation.83 | convolution fusion | flops 2014838784 | bytes 6750208 | tf_op jit(solution)/shard_map/dot_general | solution.py:16
  564.6 6.2 fusion.45
  577.8 36.9 %psum.7 = f32[2048]{0:T(1024)} all-reduce(f32[2048]{0:T(1024)S(1)} %get-tuple-element.650), channel_id=1, replica_groups=mesh['dp'=4,'ctx'=8] {'dp','ctx'}, use_global_device_ids=true, to_apply=%region_18.21 | all-reduce | flops 2048 | bytes 16384 | tf_op jit(solution)/shard_map/psum | solution.py:189
  (168 shorter events, 181.0 us)
Async XLA Ops:
  7.2 280.1 %copy-start = (bf16[1,768,2048]{2,1,0:T(8,128)(2,1)S(1)}, bf16[1,768,2048]{2,1,0:T(8,128)(2,1)}, u32[]{:S(2)}) copy-start(bf16[1,768,2048]{2,1,0:T(8,128)(2,1)} %param.30) | copy-start | bytes 9437188
  72.7 6.6 %copy-start.2 = (f32[2,512,128,16]{2,1,3,0:T(8,128)S(1)}, f32[2,512,128,16]{2,1,3,0:T(8,128)}, u32[]{:S(2)}) copy-start(f32[2,512,128,16]{2,1,3,0:T(8,128)} %get-tuple-element.936) | copy-start | bytes 25165828 | tf_op jit(solution)/shard_map/while
  100.7 6.9 %copy-start.2 = (f32[2,512,128,16]{2,1,3,0:T(8,128)S(1)}, f32[2,512,128,16]{2,1,3,0:T(8,128)}, u32[]{:S(2)}) copy-start(f32[2,512,128,16]{2,1,3,0:T(8,128)} %get-tuple-element.936) | copy-start | bytes 25165828 | tf_op jit(solution)/shard_map/while
  109.3 10.7 %copy-start.17 = (s32[128,4]{0,1:T(4,128)S(1)}, s32[128,4]{0,1:T(4,128)}, u32[]{:S(2)}) copy-start(s32[128,4]{0,1:T(4,128)} %param.25) | copy-start | bytes 6148
  109.3 11.5 %copy-start.16 = (f32[2048]{0:T(1024)S(1)}, f32[2048]{0:T(1024)}, u32[]{:S(2)}) copy-start(f32[2048]{0:T(1024)} %param.27) | copy-start | bytes 24580
  129.4 76.3 %all-to-all-start = ((bf16[32,20,2048]{2,1,0:T(8,128)(2,1)}), bf16[32,20,2048]{2,1,0:T(8,128)(2,1)}, u32[]{:S(2)}, u32[]{:S(2)}) async-start(bf16[32,20,2048]{2,1,0:T(8,128)(2,1)} %reshape.246), calls=%async_computation | async-start | bytes 6291456 | tf_op jit(solution)/shard_map/all_to_all | solution.py:42
  205.7 76.3 %all-to-all-start.2 = ((bf16[32,20,2048]{2,1,0:T(8,128)(2,1)}), bf16[32,20,2048]{2,1,0:T(8,128)(2,1)}, u32[]{:S(2)}, u32[]{:S(2)}) async-start(bf16[32,20,2048]{2,1,0:T(8,128)(2,1)} %reshape.251), calls=%async_computation.2 | async-start | bytes 6291456 | tf_op jit(solution)/shard_map/all_to_all | solution.py:42
  214.6 6.3 %copy-start.13 = (bf16[640,2048]{1,0:T(8,128)(2,1)S(1)}, bf16[640,2048]{1,0:T(8,128)(2,1)}, u32[]{:S(2)}) copy-start(bf16[640,2048]{1,0:T(8,128)(2,1)} %reshape.247) | copy-start | bytes 7864324
  214.6 6.3 %copy-start.19 = (bf16[1,2048,768]{2,1,0:T(8,128)(2,1)S(1)}, bf16[1,2048,768]{2,1,0:T(8,128)(2,1)}, u32[]{:S(2)}) copy-start(bf16[1,2048,768]{2,1,0:T(8,128)(2,1)} %param.28) | copy-start | bytes 9437188
  287.3 6.9 %copy-start.20 = (bf16[1,2048,768]{2,1,0:T(8,128)(2,1)S(1)}, bf16[1,2048,768]{2,1,0:T(8,128)(2,1)}, u32[]{:S(2)}) copy-start(bf16[1,2048,768]{2,1,0:T(8,128)(2,1)} %param.28) | copy-start | bytes 9437188
  305.6 76.2 %all-to-all-start.3 = ((bf16[32,20,2048]{2,1,0:T(8,128)(2,1)}), bf16[32,20,2048]{2,1,0:T(8,128)(2,1)}, u32[]{:S(2)}, u32[]{:S(2)}) async-start(bf16[32,20,2048]{2,1,0:T(8,128)(2,1)} %reshape.253), calls=%async_computation.3 | async-start | bytes 6291456 | tf_op jit(solution)/shard_map/all_to_all | solution.py:42
  381.8 76.2 %all-to-all-start.1 = ((bf16[32,20,2048]{2,1,0:T(8,128)(2,1)}), bf16[32,20,2048]{2,1,0:T(8,128)(2,1)}, u32[]{:S(2)}, u32[]{:S(2)}) async-start(bf16[32,20,2048]{2,1,0:T(8,128)(2,1)} %reshape.248), calls=%async_computation.1 | async-start | bytes 6291456 | tf_op jit(solution)/shard_map/all_to_all | solution.py:42
  385.4 229.4 %reduce-scatter.3.cloned.1.call-start = ((), (), s32[]{:S(2)}) async-start(), calls=%async_computation.6 | async-start | bytes 294912 | tf_op jit(solution)/shard_map/reduce_scatter | solution.py:244
  487.7 4.9 copy-start.12
  493.5 7.6 %copy-start.5 = (bf16[128,2,16,64]{0,3,2,1:T(8,128)(2,1)S(1)}, bf16[128,2,16,64]{0,3,2,1:T(8,128)(2,1)}, u32[]{:S(2)}) copy-start(bf16[128,2,16,64]{0,3,2,1:T(8,128)(2,1)} %get-tuple-element.1058) | copy-start | bytes 1572868
  493.6 7.6 %copy-start.6 = (f32[128,2,16,64]{0,3,2,1:T(8,128)S(1)}, f32[128,2,16,64]{0,3,2,1:T(8,128)}, u32[]{:S(2)}) copy-start(f32[128,2,16,64]{0,3,2,1:T(8,128)} %custom-call.3) | copy-start | bytes 3145732
  493.6 7.6 %copy-start.9 = (s32[16]{0:T(128)S(1)}, s32[16]{0:T(128)}, u32[]{:S(2)}) copy-start(s32[16]{0:T(128)} %get-tuple-element.1059) | copy-start | bytes 196
  493.6 7.6 %copy-start.10 = (bf16[1024,128]{0,1:T(8,128)(2,1)S(1)}, bf16[1024,128]{0,1:T(8,128)(2,1)}, u32[]{:S(2)}) copy-start(bf16[1024,128]{0,1:T(8,128)(2,1)} %get-tuple-element.1067) | copy-start | bytes 786436
  557.8 6.8 %copy-start.7 = (f32[128,2,16,64]{0,3,2,1:T(8,128)}, f32[128,2,16,64]{0,3,2,1:T(8,128)S(1)}, u32[]{:S(2)}) copy-start(f32[128,2,16,64]{0,3,2,1:T(8,128)S(1)} %get-tuple-element.530) | copy-start | bytes 3145732
  557.8 6.8 %copy-start.25 = (bf16[640,768]{1,0:T(8,128)(2,1)S(1)}, bf16[640,768]{1,0:T(8,128)(2,1)}, u32[]{:S(2)}) copy-start(bf16[640,768]{1,0:T(8,128)(2,1)} %copy-done.24) | copy-start | bytes 2949124
  557.8 59.5 %reduce-scatter.5.cloned.1.call-start = ((), (), s32[]{:S(2)}) async-start(), calls=%async_computation.7 | async-start | bytes 294912 | tf_op jit(solution)/shard_map/reduce_scatter | solution.py:247
  564.6 6.2 %copy-start.14 = (bf16[640,2048]{1,0:T(8,128)(2,1)S(1)}, bf16[640,2048]{1,0:T(8,128)(2,1)}, u32[]{:S(2)}) copy-start(bf16[640,2048]{1,0:T(8,128)(2,1)} %reshape.252) | copy-start | bytes 7864324
  564.6 6.2 copy-start.23
  570.9 46.4 %copy-start.1 = (bf16[1,768,2048]{2,1,0:T(8,128)(2,1)S(1)}, bf16[1,768,2048]{2,1,0:T(8,128)(2,1)}, u32[]{:S(2)}) copy-start(bf16[1,768,2048]{2,1,0:T(8,128)(2,1)} %param.30) | copy-start | bytes 9437188
  (11 other events, 26.7 us)
Sparse Core Ops, SparseCore 0:
  557.9 27.8 reduce-scatter.2
  588.7 28.5 reduce-scatter.4
where the time goes:
time: 635 us; the launch traced here: 624 us
  waiting for transfers between devices  251 us (40%)
  matrix products  105 us (17%)
  local copies, waits for them, and re-layouts  86.4 us (14%)
  other arithmetic  86 us (14%)
  blocking collectives  65.7 us (10%)
  starting transfers between devices  14.9 us (2%)
  between operations  14.6 us (2%)
    all_to_all x4, waiting for transfers between devices, trade_rows(): lax.all_to_all(buffer, ('dp', 'ctx'), split_axis=0, concat_axis=0, tiled=...  249 us
    add x4, other arithmetic, key_places(): jnp.take(block_order, rows_here // block_rows) * block_rows  40.5 us
    psum x1, blocking collectives, local(): lax.psum(jnp.sum(grad_normed * hidden_f * inv_rms, axis=0), ('dp', 'ctx'))  36.9 us
    dot_general x3, matrix products, contract_rows(): lax.dot_general(left_side, right_side, (((0,), (0,)), ((), ())), preferre...  17 us
    all_gather x1, blocking collectives, local(): lax.all_gather(keys, 'ctx', axis=0, tiled=True)  14.8 us
    all_to_all x4, starting transfers between devices, trade_rows(): lax.all_to_all(buffer, ('dp', 'ctx'), split_axis=0, concat_axis=0, tiled=...  14.5 us
    all_gather x1, blocking collectives, local(): lax.all_gather(values, 'ctx', axis=0, tiled=True)  14.1 us
    dot_general x4, matrix products, scores_for(): jnp.einsum('tkgd,pkd->kgtp', query_heads, key_heads, preferred_element_ty...  13.7 us
  transfers between devices with their start and end apart: 6, of which 5 were waited for; matrix products, arithmetic and copies ran while one was open for 10% of the time, Pallas kernels for 0%

commit v1 on v0

v1 whole, which is shorter than its diff:
```python
import functools

import jax
import jax.numpy as jnp
from jax import lax
from jax.experimental import pallas as pl
from jax.experimental.pallas import tpu as pltpu
from jax.sharding import PartitionSpec as P

DH = 64
NEG_BIG = -1e30
EPSILON = 1e-06
F32 = jnp.float32
BF16 = jnp.bfloat16
VMEM_BYTES = 48 * 1024 * 1024


def dot_nn(a, b):
    return lax.dot_general(a, b, (((1,), (0,)), ((), ())), preferred_element_type=F32)


def dot_nt(a, b):
    return lax.dot_general(a, b, (((1,), (1,)), ((), ())), preferred_element_type=F32)


def dot_tn(a, b):
    return lax.dot_general(a, b, (((0,), (0,)), ((), ())), preferred_element_type=F32)


def twin(block, head):
    lane = lax.broadcasted_iota(jnp.int32, block.shape, 1)
    turned = jnp.concatenate([block[:, DH:], block[:, :DH]], axis=1)
    return jnp.where((lane < DH) == (head == 0), block, turned)


def spread(block):
    lane = lax.broadcasted_iota(jnp.int32, block.shape, 1)
    zero = jnp.zeros_like(block)
    return jnp.concatenate(
        [jnp.where(lane < DH, block, zero), jnp.where(lane >= DH, block, zero)], axis=0
    )


def unspread(stacked):
    rows = stacked.shape[0] // 2
    lane = lax.broadcasted_iota(jnp.int32, (rows, stacked.shape[1]), 1)
    return jnp.where(lane < DH, stacked[:rows], stacked[rows:])


def prepare(kv_ref, qplace_ref, kplace_ref, bias, twins):
    width = kv_ref.shape[1] // 2
    bias[...] = jnp.where(qplace_ref[...] >= kplace_ref[...], 0.0, NEG_BIG).astype(F32)
    for part in range(2):
        block = kv_ref[:, part * width : (part + 1) * width].astype(F32)
        for head in range(2):
            twins[part, head] = twin(block, head).astype(BF16)


def masked_scores(q2, keys2, bias):
    scores = dot_nt(q2, keys2) * (DH**-0.5)
    rows = bias.shape[0]
    return jnp.concatenate([scores[:rows] + bias[...], scores[rows:] + bias[...]], axis=0)


def forward_kernel(pairs, q_ref, kv_ref, qplace_ref, kplace_ref, out_ref, lse_ref, bias, twins):
    step = pl.program_id(0)

    @pl.when(step == 0)
    def _():
        prepare(kv_ref, qplace_ref, kplace_ref, bias, twins)

    group = step // (pairs // 2)
    scores = masked_scores(spread(q_ref[...]), twins[0, group], bias)
    top = jnp.max(scores, axis=1, keepdims=True)
    weights = jnp.exp(scores - top)
    total = jnp.sum(weights, axis=1, keepdims=True)
    mixed = dot_nn(weights.astype(BF16), twins[1, group])
    out_ref[...] = unspread(mixed / total).astype(BF16)
    lse_ref[0] = top + jnp.log(total)


def backward_kernel(
    pairs,
    q_ref,
    kv_ref,
    qplace_ref,
    kplace_ref,
    att_ref,
    lse_ref,
    grad_ref,
    dq_ref,
    dkv_ref,
    bias,
    twins,
    sums,
):
    step = pl.program_id(0)

    @pl.when(step == 0)
    def _():
        prepare(kv_ref, qplace_ref, kplace_ref, bias, twins)
        sums[...] = jnp.zeros_like(sums)

    group = step // (pairs // 2)
    q2 = spread(q_ref[...])
    g2 = spread(grad_ref[...])
    keys2 = twins[0, group]
    probs = jnp.exp(masked_scores(q2, keys2, bias) - lse_ref[0])
    product = grad_ref[...].astype(F32) * att_ref[...].astype(F32)
    row_dots = jnp.sum(spread(product), axis=1, keepdims=True)
    grad_probs = dot_nt(g2, twins[1, group])
    grad_scores = (probs * (grad_probs - row_dots) * (DH**-0.5)).astype(BF16)
    dq_ref[...] = unspread(dot_nn(grad_scores, keys2)).astype(BF16)
    sums[0, group] += dot_tn(grad_scores, q2)
    sums[1, group] += dot_tn(probs.astype(BF16), g2)

    @pl.when(step == pairs - 1)
    def _():
        width = dkv_ref.shape[1] // 2
        for part in range(2):
            folded = []
            for head in range(2):
                both = sums[part, head]
                folded.append(
                    both + jnp.concatenate([both[:, DH:], both[:, :DH]], axis=1)
                )
            lane = lax.broadcasted_iota(jnp.int32, folded[0].shape, 1)
            dkv_ref[:, part * width : (part + 1) * width] = jnp.where(
                lane < DH, folded[0], folded[1]
            ).astype(BF16)


def attention_specs(rows, seq):
    pair = pl.BlockSpec((rows, 2 * DH), lambda i: (0, i))
    lse = pl.BlockSpec((1, 2 * rows, 1), lambda i: (i, 0, 0))
    full = lambda shape: pl.BlockSpec(shape, lambda i: (0, 0))
    common = [pair, full((seq, 4 * DH)), full((rows, 1)), full((1, seq))]
    scratch = [pltpu.VMEM((rows, seq), F32), pltpu.VMEM((2, 2, seq, 2 * DH), BF16)]
    return pair, lse, full, common, scratch


def attend_forward(queries, kv, qplace, kplace):
    rows, width = queries.shape
    seq = kv.shape[0]
    pairs = width // (2 * DH)
    pair, lse, full, common, scratch = attention_specs(rows, seq)
    return pl.pallas_call(
        functools.partial(forward_kernel, pairs),
        grid=(pairs,),
        in_specs=common,
        out_specs=[pair, lse],
        out_shape=[
            jax.ShapeDtypeStruct((rows, width), BF16),
            jax.ShapeDtypeStruct((pairs, 2 * rows, 1), F32),
        ],
        scratch_shapes=scratch,
        compiler_params=pltpu.CompilerParams(vmem_limit_bytes=VMEM_BYTES),
        cost_estimate=pl.CostEstimate(
            flops=16 * rows * width * seq, bytes_accessed=40_000_000, transcendentals=0
        ),
        name="attend_forward",
    )(queries, kv, qplace, kplace)


def attend_backward(queries, kv, qplace, kplace, attended, log_totals, grads):
    rows, width = queries.shape
    seq = kv.shape[0]
    pairs = width // (2 * DH)
    pair, lse, full, common, scratch = attention_specs(rows, seq)
    return pl.pallas_call(
        functools.partial(backward_kernel, pairs),
        grid=(pairs,),
        in_specs=common + [pair, lse, pair],
        out_specs=[pair, full((seq, 4 * DH))],
        out_shape=[
            jax.ShapeDtypeStruct((rows, width), BF16),
            jax.ShapeDtypeStruct((seq, 4 * DH), BF16),
        ],
        scratch_shapes=scratch + [pltpu.VMEM((2, 2, seq, 2 * DH), F32)],
        compiler_params=pltpu.CompilerParams(vmem_limit_bytes=VMEM_BYTES),
        cost_estimate=pl.CostEstimate(
            flops=40 * rows * width * seq, bytes_accessed=80_000_000, transcendentals=0
        ),
        name="attend_backward",
    )(queries, kv, qplace, kplace, attended, log_totals, grads)


def trade_rows(buffer):
    return lax.all_to_all(buffer, ("dp", "ctx"), split_axis=0, concat_axis=0, tiled=True)


def local(
    resid,
    queries,
    keys,
    values,
    block_order,
    routes,
    route_weights,
    norm_gain,
    w_gate,
    w_up,
    w_down,
    cotangent,
):
    tok_rows, model_width = resid.shape
    block_rows = tok_rows // 2
    ctx_count = lax.axis_size("ctx")
    seq_rows = tok_rows * ctx_count
    top_count = routes.shape[1]
    expert_count = lax.axis_size("dp") * ctx_count * w_gate.shape[0]
    capacity = max(2, 5 * tok_rows * top_count // (4 * expert_count))
    room = -(-capacity // 8) * 8
    slots_all = expert_count * room

    experts = jnp.arange(expert_count, dtype=jnp.int32)
    named = (routes[:, :, None] == experts[None, None, :]).astype(F32)
    token = jnp.arange(tok_rows, dtype=jnp.int32)
    earlier = (token[:, None] > token[None, :]).astype(BF16)
    before = dot_nn(earlier, jnp.sum(named, axis=1).astype(BF16))
    rank = jnp.sum(named * before[:, None, :], axis=2).astype(jnp.int32)
    flat_slots = routes * room + rank
    slot_ids = jnp.arange(slots_all, dtype=jnp.int32)
    slot_map = jnp.zeros((slots_all, tok_rows), F32)
    weight_map = jnp.zeros((slots_all, tok_rows), F32)
    for k in range(top_count):
        chosen = flat_slots[:, k][None, :] == slot_ids[:, None]
        slot_map = slot_map + chosen.astype(F32)
        weight_map = weight_map + jnp.where(chosen, route_weights[:, k][None, :], 0.0)
    dispatch = slot_map.astype(BF16)
    slot_weights = jnp.sum(weight_map, axis=1, keepdims=True)
    weight_high = weight_map.astype(BF16)
    weight_low = (weight_map - weight_high.astype(F32)).astype(BF16)
    buffer_shape = (expert_count, room, model_width)

    grad_send = (slot_weights * dot_nn(dispatch, cotangent)).astype(BF16).reshape(buffer_shape)
    kv = lax.all_gather(jnp.concatenate([keys, values], axis=1), "ctx", axis=0, tiled=True)
    grad_recv = trade_rows(grad_send).reshape(-1, model_width)

    within = jnp.arange(block_rows, dtype=jnp.int32)
    kplace = (block_order[:, None] * block_rows + within[None, :]).reshape(1, seq_rows)
    own_blocks = lax.dynamic_slice_in_dim(block_order, 2 * lax.axis_index("ctx"), 2, 0)
    qplace = (own_blocks[:, None] * block_rows + within[None, :]).reshape(tok_rows, 1)
    attended, log_totals = attend_forward(queries, kv, qplace, kplace)

    hidden = (resid.astype(F32) + attended.astype(F32)).astype(BF16)
    hidden_f = hidden.astype(F32)
    inv_rms = lax.rsqrt(jnp.mean(hidden_f * hidden_f, axis=-1, keepdims=True) + EPSILON)
    normed = (hidden_f * inv_rms * norm_gain).astype(BF16)
    send_rows = dot_nn(dispatch, normed).astype(BF16).reshape(buffer_shape)
    received = trade_rows(send_rows).reshape(-1, model_width)

    gate_w, up_w, down_w = w_gate[0], w_up[0], w_down[0]
    gate_lin = dot_nn(received, gate_w)
    up_lin = dot_nn(received, up_w)
    gate_sig = jax.nn.sigmoid(gate_lin)
    gate_act = gate_lin * gate_sig
    hidden_act = (gate_act * up_lin).astype(BF16)
    grad_act = dot_nt(grad_recv, down_w)
    grad_gate = (grad_act * up_lin * gate_sig * (1.0 + gate_lin * (1.0 - gate_sig))).astype(BF16)
    grad_up = (grad_act * gate_act).astype(BF16)
    grad_input = (dot_nt(grad_gate, gate_w) + dot_nt(grad_up, up_w)).astype(BF16)
    grad_back = trade_rows(grad_input.reshape(buffer_shape)).reshape(-1, model_width)
    produced = dot_nn(hidden_act, down_w).astype(BF16)
    produced, grad_back = lax.optimization_barrier((produced, grad_back))
    returned = trade_rows(produced.reshape(buffer_shape)).reshape(-1, model_width)
    d_w_gate = dot_tn(received, grad_gate).astype(BF16)[None]
    d_w_up = dot_tn(received, grad_up).astype(BF16)[None]
    d_w_down = dot_tn(hidden_act, grad_recv).astype(BF16)[None]

    grad_normed = dot_tn(dispatch, grad_back)
    grad_scaled = grad_normed * norm_gain
    grad_hidden = inv_rms * grad_scaled - hidden_f * inv_rms * inv_rms * inv_rms * jnp.mean(
        grad_scaled * hidden_f, axis=-1, keepdims=True
    )
    d_resid = (cotangent.astype(F32) + grad_hidden).astype(BF16)
    gain_terms = jnp.sum(grad_normed * hidden_f * inv_rms, axis=0)
    gains = lax.all_gather(gain_terms.reshape(-1, 128), ("dp", "ctx"), axis=0, tiled=False)
    d_gain = jnp.sum(gains, axis=0).reshape(-1)

    d_queries, d_kv = attend_backward(
        queries, kv, qplace, kplace, attended, log_totals, d_resid
    )
    kv_terms = lax.all_to_all(
        d_kv.reshape(ctx_count, tok_rows, -1), "ctx", split_axis=0, concat_axis=0, tiled=True
    )
    d_kv_mine = jnp.sum(kv_terms.astype(F32), axis=0).astype(BF16)

    mixed = dot_tn(weight_high, returned) + dot_tn(weight_low, returned)
    layer_out = (hidden_f + mixed).astype(BF16)
    width = keys.shape[1]
    return (
        layer_out,
        d_resid,
        d_queries,
        d_kv_mine[:, :width],
        d_kv_mine[:, width:],
        d_gain,
        d_w_gate,
        d_w_up,
        d_w_down,
    )


def solution(mesh):
    rows = P(("dp", "ctx"), None)
    stacks = P(("dp", "ctx"), None, None)
    return jax.shard_map(
        local,
        mesh=mesh,
        in_specs=(rows, rows, rows, rows, P(), rows, rows, P(), stacks, stacks, stacks, rows),
        out_specs=(rows, rows, rows, rows, rows, P(), stacks, stacks, stacks),
        check_vma=False,
    )
```

time: 635 us -> 441 us (0.69); the launches traced: 624 us -> 440 us
  local copies, waits for them, and re-layouts: 86.4 us -> 6.03 us
  other arithmetic: 86 us -> 6.23 us
  waiting for transfers between devices: 251 us -> 195 us
  blocking collectives: 65.7 us -> 119 us
  matrix products: 105 us -> 67.2 us
  Pallas kernels: 0 us -> 29.3 us
  between operations: 14.6 us -> 0.91 us
    all_gather x2, blocking collectives: 28.8 us -> 101 us  [the longest x1 83.4 us: local(): lax.all_gather(gain_terms.reshape(-1, 128), ('dp', 'ctx'), axis=0, tiled=...]
    all_to_all x4, waiting for transfers between devices: 249 us -> 195 us  [trade_rows(): lax.all_to_all(buffer, ('dp', 'ctx'), split_axis=0, concat_axis=0, tiled=...]
    add x9 -> x3, other arithmetic: 50.8 us -> 0.83 us  [the longest x1 0.69 us: local(): flat_slots = routes * room + rank]
    reshape x9 -> x0, local copies, waits for them, and re-layouts: 38.3 us -> none  [the longest x1 5.2 us: local(): grad_recv = trade_rows(grad_send).reshape(-1, model_width)]
    dot_general x26 -> x15, matrix products: 105 us -> 67.2 us  [the longest x6 27.9 us: dot_tn(): lax.dot_general(a, b, (((0,), (0,)), ((), ())), preferred_element_type=F32)]
    psum x1 -> x0, blocking collectives: 36.9 us -> none  [local(): lax.psum(jnp.sum(grad_normed * hidden_f * inv_rms, axis=0), ('dp', 'ctx'))]
    pallas_call x0 -> x2, Pallas kernels: none -> 29.3 us  [the longest x1 17.7 us: attend_backward(): pl.pallas_call(functools.partial(backward_kernel, pairs), grid=(pairs,),...]
    all_to_all x0 -> x1, blocking collectives: none -> 17.8 us  [local(): lax.all_to_all(d_kv.reshape(ctx_count, tok_rows, -1), 'ctx', split_axis=0...]
  transfers between devices with their start and end apart: 6 -> 4, of which waited for: 5 -> 3; matrix products, arithmetic and copies ran while one was open for 10% -> 10% of each run, Pallas kernels for 0% -> 0%
where the time goes in v1:
time: 441 us; the launch traced here: 440 us
  waiting for transfers between devices  195 us (44%)
  blocking collectives  119 us (27%)
  matrix products  67.2 us (15%)
  Pallas kernels  29.3 us (7%)
  starting transfers between devices  16.8 us (4%)
  other arithmetic  6.23 us (1%)
  local copies, waits for them, and re-layouts  6.03 us (1%)
    all_to_all x4, waiting for transfers between devices, trade_rows(): lax.all_to_all(buffer, ('dp', 'ctx'), split_axis=0, concat_axis=0, tiled=...  195 us
    all_gather x1, blocking collectives, local(): lax.all_gather(gain_terms.reshape(-1, 128), ('dp', 'ctx'), axis=0, tiled=...  83.4 us
    dot_general x6, matrix products, dot_tn(): lax.dot_general(a, b, (((0,), (0,)), ((), ())), preferred_element_type=F32)  27.9 us
    dot_general x6, matrix products, dot_nn(): lax.dot_general(a, b, (((1,), (0,)), ((), ())), preferred_element_type=F32)  24.8 us
    all_to_all x1, blocking collectives, local(): lax.all_to_all(d_kv.reshape(ctx_count, tok_rows, -1), 'ctx', split_axis=0...  17.8 us
    pallas_call x1, Pallas kernels, attend_backward(): pl.pallas_call(functools.partial(backward_kernel, pairs), grid=(pairs,),...  17.7 us
    all_gather x1, blocking collectives, local(): lax.all_gather(jnp.concatenate([keys, values], axis=1), 'ctx', axis=0, ti...  17.6 us
    all_to_all x4, starting transfers between devices, trade_rows(): lax.all_to_all(buffer, ('dp', 'ctx'), split_axis=0, concat_axis=0, tiled=...  16.8 us
  transfers between devices with their start and end apart: 4, of which 3 were waited for; matrix products, arithmetic and copies ran while one was open for 10% of the time, Pallas kernels for 0%

profile of v1, /device:TPU:0, one launch (start us, length us, event | category | flops | bytes accessed | tf_op | source)
XLA Modules:
  0.0 440.4 jit_solution(3030309784169530639)
XLA Ops:
  5.5 17.6 %all_gather.6.kv_ref = bf16[1024,256]{1,0:T(8,128)(2,1)} all-gather(bf16[128,256]{1,0:T(8,128)(2,1)S(1)} %pad_maximum_fusion), channel_id=1, replica_groups=mesh['dp'=4,'ctx'=8] {'ctx'}, dimensions={0}, use_global_device_ids=true | all-gather | bytes 589824 | tf_op jit(solution)/shard_map/all_gather | solution.py:237
  25.3 11.5 %attend_forward.1 = (bf16[128,2048]{1,0:T(8,128)(2,1)S(1)}, f32[16,256,1]{2,1,0:T(8,128)S(1)}) custom-call(bf16[128,2048]{1,0:T(8,128)(2,1)S(1)} %copy-done.7, bf16[1024,256]{1,0:T(8,128)(2,1)S(1)} %copy-done.3, s32[128,1]{1,0:T(8,128)S(1)} %add.127.qplace_ref, s32[1,1024]{1,0:T(1,128)S(1)} %add.110.kplace_ref), custom_call_target="tpu_custom_call" | custom-call | flops 4294967296 | bytes 40000000 | tf_op jit(solution)/shard_map/attend_forward/pallas_call | solution.py:147
  42.8 5.6 %all-to-all-start = ((bf16[32,24,2048]{2,1,0:T(8,128)(2,1)}), bf16[32,24,2048]{2,1,0:T(8,128)(2,1)}, u32[]{:S(2)}, u32[]{:S(2)}) async-start(bf16[32,24,2048]{2,1,0:T(8,128)(2,1)} %bitcast.68), calls=%async_computation | async-start | bytes 6291456 | tf_op jit(solution)/shard_map/all_to_all | solution.py:189
  48.7 3.7 multiply_convert_fusion
  52.4 68.6 %all-to-all-done = bf16[32,24,2048]{2,1,0:T(8,128)(2,1)} async-done(((bf16[32,24,2048]{2,1,0:T(8,128)(2,1)}), bf16[32,24,2048]{2,1,0:T(8,128)(2,1)}, u32[]{:S(2)}, u32[]{:S(2)}) %all-to-all-start) | async-done | bytes 3145760 | tf_op jit(solution)/shard_map/all_to_all | solution.py:189
  121.1 3.7 all-to-all-start.1
  124.8 7.0 %fusion.4 = f32[768,768]{1,0:T(8,128)} fusion(bf16[768,2048]{1,0:T(8,128)(2,1)} %bitcast.9, bf16[1,2048,768]{2,1,0:T(8,128)(2,1)} %param.21), kind=kOutput, calls=%fused_computation.11 | convolution fusion | flops 2415919104 | bytes 8650752 | tf_op jit(solution)/shard_map/dot_general | solution.py:19
  131.8 5.9 %fusion.8 = f32[768,768]{1,0:T(8,128)} fusion(bf16[768,2048]{1,0:T(8,128)(2,1)} %bitcast.9, bf16[1,2048,768]{2,1,0:T(8,128)(2,1)S(1)} %copy-done.17), kind=kOutput, calls=%fused_computation.15 | convolution fusion | flops 2415919104 | bytes 8650752 | tf_op jit(solution)/shard_map/dot_general | solution.py:19
  137.7 59.5 %all-to-all-done.1 = bf16[32,24,2048]{2,1,0:T(8,128)(2,1)} async-done(((bf16[32,24,2048]{2,1,0:T(8,128)(2,1)}), bf16[32,24,2048]{2,1,0:T(8,128)(2,1)}, u32[]{:S(2)}, u32[]{:S(2)}) %all-to-all-start.1) | async-done | bytes 3145760 | tf_op jit(solution)/shard_map/all_to_all | solution.py:189
  197.2 7.9 %multiply_convert_fusion.1 = (bf16[768,768]{1,0:T(8,128)(2,1)S(1)}, bf16[768,768]{1,0:T(8,128)(2,1)S(1)}, bf16[768,768]{1,0:T(8,128)(2,1)}) fusion(f32[768,768]{1,0:T(8,128)} %fusion.8, f32[768,768]{1,0:T(8,128)} %fusion.4, bf16[768,2048]{1,0:T(8,128)(2,1)} %bitcast.14, bf16[1,768,2048]{2,1,0:T(8,128)(2,1)S(1)} %copy-done), kind=kOutput, calls=%fused_computation.23 | convolution fusion | flops 2424766464 | bytes 14548992 | tf_op jit(solution)/shard_map/dot_general | solution.py:23
  207.9 4.0 add_convert_fusion
  211.8 3.8 all-to-all-start.2
  215.6 5.3 %convolution_convert_fusion.3 = bf16[768,2048]{1,0:T(8,128)(2,1)} fusion(bf16[768,768]{1,0:T(8,128)(2,1)} %get-tuple-element.27, bf16[1,768,2048]{2,1,0:T(8,128)(2,1)S(1)} %copy-done), kind=kOutput, calls=%fused_computation.5 | convolution fusion | flops 2417491968 | bytes 7471104 | tf_op jit(solution)/shard_map/dot_general | solution.py:19
  220.9 67.1 %all-to-all-done.2 = bf16[32,24,2048]{2,1,0:T(8,128)(2,1)} async-done(((bf16[32,24,2048]{2,1,0:T(8,128)(2,1)}), bf16[32,24,2048]{2,1,0:T(8,128)(2,1)}, u32[]{:S(2)}, u32[]{:S(2)}) %all-to-all-start.2) | async-done | bytes 3145760 | tf_op jit(solution)/shard_map/all_to_all | solution.py:189
  288.1 3.1 fusion.27
  291.6 17.7 %attend_backward.1 = (bf16[128,2048]{1,0:T(8,128)(2,1)}, bf16[1024,256]{1,0:T(8,128)(2,1)S(1)}) custom-call(bf16[128,2048]{1,0:T(8,128)(2,1)S(1)} %copy-done.8, bf16[1024,256]{1,0:T(8,128)(2,1)S(1)} %copy-done.4, s32[128,1]{1,0:T(8,128)S(1)} %add.127.qplace_ref, s32[1,1024]{1,0:T(1,128)S(1)} %add.110.kplace_ref, bf16[128,2048]{1,0:T(8,128)(2,1)S(1)} %copy-done.6, ...), custom_call_target="tpu_custom_call" | custom-call | flops 10737418240 | bytes 80000000 | tf_op jit(solution)/shard_map/attend_backward/pallas_call | solution.py:170
  309.3 17.8 %all_to_all.25 = bf16[8,128,256]{2,1,0:T(8,128)(2,1)S(1)} all-to-all(bf16[8,128,256]{2,1,0:T(8,128)(2,1)S(1)} %bitcast.67), channel_id=1, replica_groups=mesh['dp'=4,'ctx'=8] {'ctx'}, dimensions={0} | all-to-all | bytes 1048576 | tf_op jit(solution)/shard_map/all_to_all | solution.py:284
  327.1 3.7 all-to-all-start.3
  330.8 6.3 %fusion.10 = bf16[1,2048,768]{2,1,0:T(8,128)(2,1)} fusion(bf16[768,2048]{1,0:T(8,128)(2,1)} %bitcast.9, bf16[768,768]{1,0:T(8,128)(2,1)S(1)} %copy-done.21), kind=kOutput, calls=%fused_computation.17 | convolution fusion | flops 2417491968 | bytes 7471104 | tf_op jit(solution)/shard_map/dot_general | solution.py:27
  337.1 6.3 %fusion.11 = bf16[1,2048,768]{2,1,0:T(8,128)(2,1)} fusion(bf16[768,2048]{1,0:T(8,128)(2,1)} %bitcast.9, bf16[768,768]{1,0:T(8,128)(2,1)S(1)} %copy-done.24), kind=kOutput, calls=%fused_computation.18 | convolution fusion | flops 2417491968 | bytes 7471104 | tf_op jit(solution)/shard_map/dot_general | solution.py:27
  343.5 5.9 %fusion.12 = bf16[1,768,2048]{2,1,0:T(8,128)(2,1)} fusion(bf16[768,768]{1,0:T(8,128)(2,1)S(1)} %copy-done.22, bf16[768,2048]{1,0:T(8,128)(2,1)} %bitcast.14), kind=kOutput, calls=%fused_computation.19 | convolution fusion | flops 2417491968 | bytes 7471104 | tf_op jit(solution)/shard_map/dot_general | solution.py:27
  349.4 83.4 %all_gather.7 = f32[32,16,128]{2,1,0:T(8,128)S(1)} all-gather(f32[1,16,128]{2,1,0:T(8,128)S(1)} %bitcast.72), channel_id=1, replica_groups=mesh['dp'=4,'ctx'=8] {'dp','ctx'}, dimensions={0}, use_global_device_ids=true | all-gather | bytes 270336 | tf_op jit(solution)/shard_map/all_gather | solution.py:278
  434.1 2.8 fusion.44
  436.8 3.5 fusion.14
  (74 shorter events, 17.8 us)
Async XLA Ops:
  0.6 196.6 %copy-start = (bf16[1,768,2048]{2,1,0:T(8,128)(2,1)S(1)}, bf16[1,768,2048]{2,1,0:T(8,128)(2,1)}, u32[]{:S(2)}) copy-start(bf16[1,768,2048]{2,1,0:T(8,128)(2,1)} %param.22) | copy-start | bytes 9437188
  25.3 12.9 %copy-start.14 = (bf16[128,2048]{1,0:T(8,128)(2,1)S(1)}, bf16[128,2048]{1,0:T(8,128)(2,1)}, u32[]{:S(2)}) copy-start(bf16[128,2048]{1,0:T(8,128)(2,1)} %param.12) | copy-start | bytes 1572868
  25.3 14.8 %copy-start.15 = (f32[2048]{0:T(1024)S(1)}, f32[2048]{0:T(1024)}, u32[]{:S(2)}) copy-start(f32[2048]{0:T(1024)} %param.19) | copy-start | bytes 24580
  42.8 5.6 %copy-start.16 = (f32[128,4]{0,1:T(4,128)S(1)}, f32[128,4]{0,1:T(4,128)}, u32[]{:S(2)}) copy-start(f32[128,4]{0,1:T(4,128)} %param.18) | copy-start | bytes 6148
  42.8 78.2 %all-to-all-start = ((bf16[32,24,2048]{2,1,0:T(8,128)(2,1)}), bf16[32,24,2048]{2,1,0:T(8,128)(2,1)}, u32[]{:S(2)}, u32[]{:S(2)}) async-start(bf16[32,24,2048]{2,1,0:T(8,128)(2,1)} %bitcast.68), calls=%async_computation | async-start | bytes 6291456 | tf_op jit(solution)/shard_map/all_to_all | solution.py:189
  121.1 76.2 %all-to-all-start.1 = ((bf16[32,24,2048]{2,1,0:T(8,128)(2,1)}), bf16[32,24,2048]{2,1,0:T(8,128)(2,1)}, u32[]{:S(2)}, u32[]{:S(2)}) async-start(bf16[32,24,2048]{2,1,0:T(8,128)(2,1)} %bitcast.69), calls=%async_computation.1 | async-start | bytes 6291456 | tf_op jit(solution)/shard_map/all_to_all | solution.py:189
  124.8 7.0 %copy-start.17 = (bf16[1,2048,768]{2,1,0:T(8,128)(2,1)S(1)}, bf16[1,2048,768]{2,1,0:T(8,128)(2,1)}, u32[]{:S(2)}) copy-start(bf16[1,2048,768]{2,1,0:T(8,128)(2,1)} %param.20) | copy-start | bytes 9437188
  197.2 7.9 %copy-start.18 = (bf16[1,2048,768]{2,1,0:T(8,128)(2,1)S(1)}, bf16[1,2048,768]{2,1,0:T(8,128)(2,1)}, u32[]{:S(2)}) copy-start(bf16[1,2048,768]{2,1,0:T(8,128)(2,1)} %param.20) | copy-start | bytes 9437188
  205.1 2.7 copy-start.20
  205.1 2.7 copy-start.23
  205.1 2.7 copy-start.19
  211.8 76.2 %all-to-all-start.2 = ((bf16[32,24,2048]{2,1,0:T(8,128)(2,1)}), bf16[32,24,2048]{2,1,0:T(8,128)(2,1)}, u32[]{:S(2)}, u32[]{:S(2)}) async-start(bf16[32,24,2048]{2,1,0:T(8,128)(2,1)} %bitcast.71), calls=%async_computation.2 | async-start | bytes 6291456 | tf_op jit(solution)/shard_map/all_to_all | solution.py:189
  288.0 3.1 copy-start.12
  288.0 3.1 copy-start.13
  288.0 3.6 copy-start.4
  288.0 3.6 copy-start.6
  288.0 3.6 copy-start.8
  288.0 3.6 copy-start.10
  291.6 17.8 %copy-start.2 = (bf16[128,2048]{1,0:T(8,128)(2,1)}, bf16[128,2048]{1,0:T(8,128)(2,1)S(1)}, u32[]{:S(2)}) copy-start(bf16[128,2048]{1,0:T(8,128)(2,1)S(1)} %fusion.23.grad_ref) | copy-start | bytes 1572868
  327.1 3.7 copy-start.21
  327.1 107.0 %all-to-all-start.3 = ((bf16[32,24,2048]{2,1,0:T(8,128)(2,1)}), bf16[32,24,2048]{2,1,0:T(8,128)(2,1)}, u32[]{:S(2)}, u32[]{:S(2)}) async-start(bf16[32,24,2048]{2,1,0:T(8,128)(2,1)} %bitcast.70), calls=%async_computation.3 | async-start | bytes 6291456 | tf_op jit(solution)/shard_map/all_to_all | solution.py:189
  330.8 6.3 %copy-start.24 = (bf16[768,768]{1,0:T(8,128)(2,1)S(1)}, bf16[768,768]{1,0:T(8,128)(2,1)}, u32[]{:S(2)}) copy-start(bf16[768,768]{1,0:T(8,128)(2,1)} %copy-done.23) | copy-start | bytes 3538948
  337.1 6.3 %copy-start.22 = (bf16[768,768]{1,0:T(8,128)(2,1)S(1)}, bf16[768,768]{1,0:T(8,128)(2,1)}, u32[]{:S(2)}) copy-start(bf16[768,768]{1,0:T(8,128)(2,1)} %get-tuple-element.27) | copy-start | bytes 3538948
  434.1 6.3 %copy-start.1 = (bf16[1,768,2048]{2,1,0:T(8,128)(2,1)S(1)}, bf16[1,768,2048]{2,1,0:T(8,128)(2,1)}, u32[]{:S(2)}) copy-start(bf16[1,768,2048]{2,1,0:T(8,128)(2,1)} %param.22) | copy-start | bytes 9437188
  (5 other events, 5.0 us)

commit v2 on v1

--- a/solution.py
+++ b/solution.py
@@ -1,4 +1,5 @@
 import functools
+import math
 
 import jax
 import jax.numpy as jnp
@@ -185,6 +186,41 @@
     )(queries, kv, qplace, kplace, attended, log_totals, grads)
 
 
+def regroup_kernel(moves, chunks_in, chunks_out, move_ref, in_ref, out_ref):
+    width_in = in_ref.shape[1] // chunks_in
+    width_out = out_ref.shape[1] // chunks_out
+    if chunks_in == 1:
+        for h in range(moves):
+            part = dot_nn(move_ref[h], in_ref[...])
+            out_ref[:, h * width_out : (h + 1) * width_out] = part.astype(BF16)
+    else:
+        total = dot_nn(move_ref[0], in_ref[:, :width_in])
+        for h in range(1, moves):
+            total += dot_nn(move_ref[h], in_ref[:, h * width_in : (h + 1) * width_in])
+        out_ref[...] = total.astype(BF16)
+
+
+def regroup(array, moves, chunks_in, chunks_out, name):
+    count, rows_out, rows_in = moves.shape
+    steps = array.shape[0] // rows_in
+    width_out = array.shape[1] // chunks_in * chunks_out
+    return pl.pallas_call(
+        functools.partial(regroup_kernel, count, chunks_in, chunks_out),
+        grid=(steps,),
+        in_specs=[
+            pl.BlockSpec(moves.shape, lambda i: (0, 0, 0)),
+            pl.BlockSpec((rows_in, array.shape[1]), lambda i: (i, 0)),
+        ],
+        out_specs=pl.BlockSpec((rows_out, width_out), lambda i: (i, 0)),
+        out_shape=jax.ShapeDtypeStruct((steps * rows_out, width_out), BF16),
+        compiler_params=pltpu.CompilerParams(vmem_limit_bytes=VMEM_BYTES),
+        cost_estimate=pl.CostEstimate(
+            flops=2 * array.size * rows_out, bytes_accessed=4 * array.size, transcendentals=0
+        ),
+        name=name,
+    )(moves, array)
+
+
 def trade_rows(buffer):
     return lax.all_to_all(buffer, ("dp", "ctx"), split_axis=0, concat_axis=0, tiled=True)
 
@@ -210,7 +246,7 @@
     top_count = routes.shape[1]
     expert_count = lax.axis_size("dp") * ctx_count * w_gate.shape[0]
     capacity = max(2, 5 * tok_rows * top_count // (4 * expert_count))
-    room = -(-capacity // 8) * 8
+    room = -(-(capacity + 2) // 8) * 8
     slots_all = expert_count * room
 
     experts = jnp.arange(expert_count, dtype=jnp.int32)
@@ -219,23 +255,63 @@
     earlier = (token[:, None] > token[None, :]).astype(BF16)
     before = dot_nn(earlier, jnp.sum(named, axis=1).astype(BF16))
     rank = jnp.sum(named * before[:, None, :], axis=2).astype(jnp.int32)
-    flat_slots = routes * room + rank
+    folds = 8 // math.gcd(capacity, 8)
+    fold_width = model_width // folds
+    packed_rows = folds * capacity
+    packed_shape = (expert_count, packed_rows, fold_width)
+
+    def fold(block):
+        return jnp.concatenate(
+            [block[:, h * fold_width : (h + 1) * fold_width] for h in range(folds)], axis=0
+        )
+
+    def unfold(block):
+        return jnp.concatenate(
+            [block[h * tok_rows : (h + 1) * tok_rows] for h in range(folds)], axis=1
+        )
+
+    packed_ids = jnp.arange(expert_count * packed_rows, dtype=jnp.int32)
+    packed_slot = packed_ids // packed_rows * capacity + packed_ids % capacity
+    packed_key = packed_slot * folds + packed_ids // capacity % folds
+    column_fold = jnp.arange(folds, dtype=jnp.int32)[:, None]
+    slot_map = jnp.zeros((expert_count * packed_rows, folds * tok_rows), F32)
+    slot_weights = jnp.zeros((expert_count * packed_rows, 1), F32)
     slot_ids = jnp.arange(slots_all, dtype=jnp.int32)
-    slot_map = jnp.zeros((slots_all, tok_rows), F32)
     weight_map = jnp.zeros((slots_all, tok_rows), F32)
     for k in range(top_count):
-        chosen = flat_slots[:, k][None, :] == slot_ids[:, None]
+        taken = (routes[:, k] * capacity + rank[:, k])[None, :] * folds + column_fold
+        chosen = taken.reshape(1, -1) == packed_key[:, None]
         slot_map = slot_map + chosen.astype(F32)
-        weight_map = weight_map + jnp.where(chosen, route_weights[:, k][None, :], 0.0)
+        weight = jnp.tile(route_weights[:, k], folds)[None, :]
+        slot_weights = slot_weights + jnp.sum(
+            jnp.where(chosen, weight, 0.0), axis=1, keepdims=True
+        )
+        returned_slot = (routes[:, k] * room + rank[:, k])[None, :]
+        weight_map = weight_map + jnp.where(
+            returned_slot == slot_ids[:, None], route_weights[:, k][None, :], 0.0
+        )
     dispatch = slot_map.astype(BF16)
-    slot_weights = jnp.sum(weight_map, axis=1, keepdims=True)
     weight_high = weight_map.astype(BF16)
     weight_low = (weight_map - weight_high.astype(F32)).astype(BF16)
     buffer_shape = (expert_count, room, model_width)
 
-    grad_send = (slot_weights * dot_nn(dispatch, cotangent)).astype(BF16).reshape(buffer_shape)
+    batch = 16 // math.gcd(capacity, 16)
+    row_at = jnp.arange(batch * capacity, dtype=jnp.int32)
+    first_packed = row_at // capacity * packed_rows + row_at % capacity
+    packed_at = jnp.arange(batch * packed_rows, dtype=jnp.int32)
+    unpack_moves = jnp.stack(
+        [first_packed[:, None] + h * capacity == packed_at[None, :] for h in range(folds)]
+    ).astype(BF16)
+    pack_moves = jnp.swapaxes(unpack_moves, 1, 2)
+    room_at = jnp.arange(batch * room, dtype=jnp.int32)
+    room_moves = (
+        room_at[:, None] == (row_at // capacity * room + row_at % capacity)[None, :]
+    ).astype(BF16)[None]
+
     kv = lax.all_gather(jnp.concatenate([keys, values], axis=1), "ctx", axis=0, tiled=True)
-    grad_recv = trade_rows(grad_send).reshape(-1, model_width)
+    grad_send = (slot_weights * dot_nn(dispatch, fold(cotangent))).astype(BF16)
+    kv, grad_send = lax.optimization_barrier((kv, grad_send))
+    grad_packed = trade_rows(grad_send.reshape(packed_shape)).reshape(-1, fold_width)
 
     within = jnp.arange(block_rows, dtype=jnp.int32)
     kplace = (block_order[:, None] * block_rows + within[None, :]).reshape(1, seq_rows)
@@ -247,8 +323,11 @@
     hidden_f = hidden.astype(F32)
     inv_rms = lax.rsqrt(jnp.mean(hidden_f * hidden_f, axis=-1, keepdims=True) + EPSILON)
     normed = (hidden_f * inv_rms * norm_gain).astype(BF16)
-    send_rows = dot_nn(dispatch, normed).astype(BF16).reshape(buffer_shape)
-    received = trade_rows(send_rows).reshape(-1, model_width)
+    send_rows = dot_nn(dispatch, fold(normed)).astype(BF16)
+    send_rows, grad_packed = lax.optimization_barrier((send_rows, grad_packed))
+    packed = trade_rows(send_rows.reshape(packed_shape)).reshape(-1, fold_width)
+    grad_recv = regroup(grad_packed, unpack_moves, 1, folds, "unpack_grads")
+    received = regroup(packed, unpack_moves, 1, folds, "unpack_rows")
 
     gate_w, up_w, down_w = w_gate[0], w_up[0], w_down[0]
     gate_lin = dot_nn(received, gate_w)
@@ -260,34 +339,50 @@
     grad_gate = (grad_act * up_lin * gate_sig * (1.0 + gate_lin * (1.0 - gate_sig))).astype(BF16)
     grad_up = (grad_act * gate_act).astype(BF16)
     grad_input = (dot_nt(grad_gate, gate_w) + dot_nt(grad_up, up_w)).astype(BF16)
-    grad_back = trade_rows(grad_input.reshape(buffer_shape)).reshape(-1, model_width)
-    produced = dot_nn(hidden_act, down_w).astype(BF16)
-    produced, grad_back = lax.optimization_barrier((produced, grad_back))
-    returned = trade_rows(produced.reshape(buffer_shape)).reshape(-1, model_width)
-    d_w_gate = dot_tn(received, grad_gate).astype(BF16)[None]
-    d_w_up = dot_tn(received, grad_up).astype(BF16)[None]
-    d_w_down = dot_tn(hidden_act, grad_recv).astype(BF16)[None]
-
-    grad_normed = dot_tn(dispatch, grad_back)
+    grad_input = regroup(grad_input, pack_moves, folds, 1, "pack_grads")
+    grad_back = trade_rows(grad_input.reshape(packed_shape)).reshape(-1, fold_width)
+    produced = regroup(dot_nn(hidden_act, down_w).astype(BF16), room_moves, 1, 1, "place_rows")
+    d_w_gate = dot_tn(received, grad_gate).astype(BF16)
+    d_w_up = dot_tn(received, grad_up).astype(BF16)
+    d_w_down = dot_tn(hidden_act, grad_recv).astype(BF16)
+    produced, grad_back, d_w_gate, d_w_up, d_w_down = lax.optimization_barrier(
+        (produced, grad_back, d_w_gate, d_w_up, d_w_down)
+    )
+
+    grad_normed = unfold(dot_tn(dispatch, grad_back))
     grad_scaled = grad_normed * norm_gain
     grad_hidden = inv_rms * grad_scaled - hidden_f * inv_rms * inv_rms * inv_rms * jnp.mean(
         grad_scaled * hidden_f, axis=-1, keepdims=True
     )
     d_resid = (cotangent.astype(F32) + grad_hidden).astype(BF16)
     gain_terms = jnp.sum(grad_normed * hidden_f * inv_rms, axis=0)
-    gains = lax.all_gather(gain_terms.reshape(-1, 128), ("dp", "ctx"), axis=0, tiled=False)
-    d_gain = jnp.sum(gains, axis=0).reshape(-1)
+    gain_high = gain_terms.astype(BF16)
+    gain_low = (gain_terms - gain_high.astype(F32)).astype(BF16)
+    gain_rows = jnp.broadcast_to(
+        jnp.stack([gain_high, gain_low])[None], (expert_count, 2, model_width)
+    )
+    outgoing = lax.dynamic_update_slice(
+        produced.reshape(buffer_shape), gain_rows, (0, capacity, 0)
+    )
+    outgoing, d_resid = lax.optimization_barrier((outgoing, d_resid))
+    returned = trade_rows(outgoing).reshape(-1, model_width)
 
     d_queries, d_kv = attend_backward(
         queries, kv, qplace, kplace, attended, log_totals, d_resid
     )
+    d_kv, returned = lax.optimization_barrier((d_kv, returned))
     kv_terms = lax.all_to_all(
         d_kv.reshape(ctx_count, tok_rows, -1), "ctx", split_axis=0, concat_axis=0, tiled=True
     )
     d_kv_mine = jnp.sum(kv_terms.astype(F32), axis=0).astype(BF16)
 
-    mixed = dot_tn(weight_high, returned) + dot_tn(weight_low, returned)
-    layer_out = (hidden_f + mixed).astype(BF16)
+    place = slot_ids % room
+    gain_slots = ((place >= capacity) & (place < capacity + 2)).astype(BF16)
+    gain_columns = jnp.broadcast_to(gain_slots[:, None], (slots_all, 128))
+    readers = jnp.concatenate([weight_high, weight_low, gain_columns], axis=1)
+    combined = dot_tn(readers, returned)
+    layer_out = (hidden_f + combined[:tok_rows] + combined[tok_rows : 2 * tok_rows]).astype(BF16)
+    d_gain = combined[2 * tok_rows]
     width = keys.shape[1]
     return (
         layer_out,
@@ -296,9 +391,9 @@
         d_kv_mine[:, :width],
         d_kv_mine[:, width:],
         d_gain,
-        d_w_gate,
-        d_w_up,
-        d_w_down,
+        d_w_gate[None],
+        d_w_up[None],
+        d_w_down[None],
     )
 
 

time: 441 us -> 352 us (0.80)
  blocking collectives: 119 us -> 17.6 us
  matrix products: 67.2 us -> 40.6 us
  Pallas kernels: 29.3 us -> 46.6 us
  local copies, waits for them, and re-layouts: 6.03 us -> 16.9 us
    all_gather x1 -> x0, blocking collectives: 83.4 us -> none  [local(): lax.all_gather(gain_terms.reshape(-1, 128), ('dp', 'ctx'), axis=0, tiled=...]
    all_to_all x1 -> x0, blocking collectives: 17.8 us -> none  [local(): lax.all_to_all(d_kv.reshape(ctx_count, tok_rows, -1), 'ctx', split_axis=0...]
    pallas_call x0 -> x4, Pallas kernels: none -> 17.4 us  [regroup(): pl.pallas_call(functools.partial(regroup_kernel, count, chunks_in, chunks...]
    dot_general x6, matrix products: 24.8 us -> 13.3 us  [dot_nn(): lax.dot_general(a, b, (((1,), (0,)), ((), ())), preferred_element_type=F32)]
    all_to_all x0 -> x1, waiting for transfers between devices: none -> 10 us  [local(): lax.all_to_all(d_kv.reshape(ctx_count, tok_rows, -1), 'ctx', split_axis=0...]
    dot_general x6 -> x5, matrix products: 27.9 us -> 18.8 us  [dot_tn(): lax.dot_general(a, b, (((0,), (0,)), ((), ())), preferred_element_type=F32)]
    all_to_all x4, waiting for transfers between devices: 195 us -> 188 us  [trade_rows(): lax.all_to_all(buffer, ('dp', 'ctx'), split_axis=0, concat_axis=0, tiled=...]
    unnamed x50 -> x64, local copies, waits for them, and re-layouts: 5.17 us -> 12.2 us
  transfers between devices with their start and end apart: 4 -> 5, of which waited for: 3 -> 5; matrix products, arithmetic and copies ran while one was open for 10% -> 7% of each run, Pallas kernels for 0% -> 11%
where the time goes in v2:
time: 352 us; the launch traced here: 351 us
  waiting for transfers between devices  198 us (56%)
  Pallas kernels  46.6 us (13%)
  matrix products  40.6 us (12%)
  starting transfers between devices  21.1 us (6%)
  blocking collectives  17.6 us (5%)
  local copies, waits for them, and re-layouts  16.9 us (5%)
  other arithmetic  9.51 us (3%)
    all_to_all x4, waiting for transfers between devices, trade_rows(): lax.all_to_all(buffer, ('dp', 'ctx'), split_axis=0, concat_axis=0, tiled=...  188 us
    dot_general x5, matrix products, dot_tn(): lax.dot_general(a, b, (((0,), (0,)), ((), ())), preferred_element_type=F32)  18.8 us
    pallas_call x1, Pallas kernels, attend_backward(): pl.pallas_call(functools.partial(backward_kernel, pairs), grid=(pairs,),...  17.7 us
    all_gather x1, blocking collectives, local(): lax.all_gather(jnp.concatenate([keys, values], axis=1), 'ctx', axis=0, ti...  17.6 us
    pallas_call x4, Pallas kernels, regroup(): pl.pallas_call(functools.partial(regroup_kernel, count, chunks_in, chunks...  17.4 us
    all_to_all x4, starting transfers between devices, trade_rows(): lax.all_to_all(buffer, ('dp', 'ctx'), split_axis=0, concat_axis=0, tiled=...  16.9 us
    dot_general x6, matrix products, dot_nn(): lax.dot_general(a, b, (((1,), (0,)), ((), ())), preferred_element_type=F32)  13.3 us
    unnamed x64, local copies, waits for them, and re-layouts  12.2 us
  transfers between devices with their start and end apart: 5, of which 5 were waited for; matrix products, arithmetic and copies ran while one was open for 7% of the time, Pallas kernels for 11%

profile of v2, /device:TPU:0, one launch (start us, length us, event | category | flops | bytes accessed | tf_op | source)
XLA Modules:
  0.0 351.1 jit_solution(14708716955303372612)
XLA Ops:
  1.6 17.6 %all_gather.3.kv_ref = bf16[1024,256]{1,0:T(8,128)(2,1)} all-gather(bf16[128,256]{1,0:T(8,128)(2,1)S(1)} %pad_maximum_fusion.1), channel_id=1, replica_groups=mesh['dp'=4,'ctx'=8] {'ctx'}, dimensions={0}, use_global_device_ids=true | all-gather | bytes 589824 | tf_op jit(solution)/shard_map/all_gather | solution.py:311
  24.5 2.8 multiply_convert_fusion
  27.3 5.6 %all-to-all-start = ((bf16[32,40,1024]{2,1,0:T(8,128)(2,1)}), bf16[32,40,1024]{2,1,0:T(8,128)(2,1)}, u32[]{:S(2)}, u32[]{:S(2)}) async-start(bf16[32,40,1024]{2,1,0:T(8,128)(2,1)} %bitcast.90), calls=%async_computation | async-start | bytes 5242880 | tf_op jit(solution)/shard_map/all_to_all | solution.py:225
  35.5 11.5 %attend_forward.1 = (bf16[128,2048]{1,0:T(8,128)(2,1)S(1)}, f32[16,256,1]{2,1,0:T(8,128)S(1)}) custom-call(bf16[128,2048]{1,0:T(8,128)(2,1)S(1)} %copy-done.14, bf16[1024,256]{1,0:T(8,128)(2,1)S(1)} %copy-done.9, s32[128,1]{1,0:T(8,128)S(1)} %add.478.qplace_ref, s32[1,1024]{1,0:T(1,128)S(1)} %add.452.kplace_ref), custom_call_target="tpu_custom_call" | custom-call | flops 4294967296 | bytes 40000000 | tf_op jit(solution)/shard_map/attend_forward/pallas_call | solution.py:148
  53.1 41.2 %all-to-all-done = bf16[32,40,1024]{2,1,0:T(8,128)(2,1)} async-done(((bf16[32,40,1024]{2,1,0:T(8,128)(2,1)}), bf16[32,40,1024]{2,1,0:T(8,128)(2,1)}, u32[]{:S(2)}, u32[]{:S(2)}) %all-to-all-start) | async-done | bytes 2621472 | tf_op jit(solution)/shard_map/all_to_all | solution.py:225
  94.3 3.7 %all-to-all-start.1 = ((bf16[32,40,1024]{2,1,0:T(8,128)(2,1)}), bf16[32,40,1024]{2,1,0:T(8,128)(2,1)}, u32[]{:S(2)}, u32[]{:S(2)}) async-start(bf16[32,40,1024]{2,1,0:T(8,128)(2,1)} %bitcast.91), calls=%async_computation.1 | async-start | bytes 5242880 | tf_op jit(solution)/shard_map/all_to_all | solution.py:225
  98.2 5.2 %unpack_grads.1 = bf16[640,2048]{1,0:T(8,128)(2,1)S(1)} custom-call(bf16[2,80,160]{2,1,0:T(8,128)(2,1)S(1)} %copy.28.move_ref, bf16[1280,1024]{1,0:T(8,128)(2,1)} %bitcast.21.in_ref), custom_call_target="tpu_custom_call" | custom-call | flops 209715200 | bytes 5242880 | tf_op jit(solution)/shard_map/unpack_grads/pallas_call | solution.py:207
  105.0 54.2 %all-to-all-done.1 = bf16[32,40,1024]{2,1,0:T(8,128)(2,1)} async-done(((bf16[32,40,1024]{2,1,0:T(8,128)(2,1)}), bf16[32,40,1024]{2,1,0:T(8,128)(2,1)}, u32[]{:S(2)}, u32[]{:S(2)}) %all-to-all-start.1) | async-done | bytes 2621472 | tf_op jit(solution)/shard_map/all_to_all | solution.py:225
  159.2 5.4 %unpack_rows.1 = bf16[640,2048]{1,0:T(8,128)(2,1)S(1)} custom-call(bf16[2,80,160]{2,1,0:T(8,128)(2,1)S(1)} %copy.28.move_ref, bf16[1280,1024]{1,0:T(8,128)(2,1)} %bitcast.23.in_ref), custom_call_target="tpu_custom_call" | custom-call | flops 209715200 | bytes 5242880 | tf_op jit(solution)/shard_map/unpack_rows/pallas_call | solution.py:207
  169.7 4.0 %multiply_convert_fusion.1 = (bf16[640,768]{1,0:T(8,128)(2,1)S(1)}, bf16[640,768]{1,0:T(8,128)(2,1)S(1)}, bf16[640,768]{1,0:T(8,128)(2,1)}) fusion(f32[640,768]{1,0:T(8,128)S(1)} %fusion.8, f32[640,768]{1,0:T(8,128)S(1)} %fusion.4, bf16[640,2048]{1,0:T(8,128)(2,1)S(1)} %copy-done.4, bf16[1,768,2048]{2,1,0:T(8,128)(2,1)S(1)} %copy-done), kind=kOutput, calls=%fused_computation.22 | convolution fusion | flops 2020638720 | bytes 12648448 | tf_op jit(solution)/shard_map/dot_general | solution.py:24
  182.3 3.7 %all-to-all-start.2 = ((bf16[32,40,1024]{2,1,0:T(8,128)(2,1)}), bf16[32,40,1024]{2,1,0:T(8,128)(2,1)}, u32[]{:S(2)}, u32[]{:S(2)}) async-start(bf16[32,40,1024]{2,1,0:T(8,128)(2,1)} %bitcast.88), calls=%async_computation.2 | async-start | bytes 5242880 | tf_op jit(solution)/shard_map/all_to_all | solution.py:225
  186.0 3.4 convolution_convert_fusion.4.in_ref
  189.5 4.2 %place_rows.1 = bf16[768,2048]{1,0:T(8,128)(2,1)} custom-call(bf16[1,96,80]{2,1,0:T(8,128)(2,1)S(1)} %fusion.51.move_ref, bf16[640,2048]{1,0:T(8,128)(2,1)S(1)} %convolution_convert_fusion.4.in_ref), custom_call_target="tpu_custom_call" | custom-call | flops 251658240 | bytes 5242880 | tf_op jit(solution)/shard_map/place_rows/pallas_call | solution.py:207
  193.7 4.1 %convolution_convert_fusion.3 = bf16[2048,768]{1,0:T(8,128)(2,1)} fusion(bf16[640,2048]{1,0:T(8,128)(2,1)S(1)} %copy-done.7, bf16[640,768]{1,0:T(8,128)(2,1)S(1)} %copy-done.28), kind=kOutput, calls=%fused_computation.5 | convolution fusion | flops 2014838784 | bytes 6750208 | tf_op jit(solution)/shard_map/dot_general | solution.py:28
  197.8 4.1 %convolution_convert_fusion.2 = bf16[2048,768]{1,0:T(8,128)(2,1)} fusion(bf16[640,2048]{1,0:T(8,128)(2,1)S(1)} %copy-done.7, bf16[640,768]{1,0:T(8,128)(2,1)S(1)} %copy-done.31), kind=kOutput, calls=%fused_computation.4 | convolution fusion | flops 2014838784 | bytes 6750208 | tf_op jit(solution)/shard_map/dot_general | solution.py:28
  201.9 4.0 %convolution_convert_fusion.1 = bf16[768,2048]{1,0:T(8,128)(2,1)} fusion(bf16[640,768]{1,0:T(8,128)(2,1)S(1)} %copy-done.29, bf16[640,2048]{1,0:T(8,128)(2,1)S(1)} %copy-done.5), kind=kOutput, calls=%fused_computation.3 | convolution fusion | flops 2014838784 | bytes 6750208 | tf_op jit(solution)/shard_map/dot_general | solution.py:28
  205.9 41.2 %all-to-all-done.2 = bf16[32,40,1024]{2,1,0:T(8,128)(2,1)} async-done(((bf16[32,40,1024]{2,1,0:T(8,128)(2,1)}), bf16[32,40,1024]{2,1,0:T(8,128)(2,1)}, u32[]{:S(2)}, u32[]{:S(2)}) %all-to-all-start.2) | async-done | bytes 2621472 | tf_op jit(solution)/shard_map/all_to_all | solution.py:225
  247.2 3.1 fusion.45
  253.4 3.8 %all-to-all-start.3 = ((bf16[32,24,2048]{2,1,0:T(8,128)(2,1)}), bf16[32,24,2048]{2,1,0:T(8,128)(2,1)}, u32[]{:S(2)}, u32[]{:S(2)}) async-start(bf16[32,24,2048]{2,1,0:T(8,128)(2,1)} %broadcast_dynamic-update-slice_fusion), calls=%async_computation.3 | async-start | bytes 6291456 | tf_op jit(solution)/shard_map/all_to_all | solution.py:225
  260.2 17.7 %attend_backward.1 = (bf16[128,2048]{1,0:T(8,128)(2,1)}, bf16[1024,256]{1,0:T(8,128)(2,1)S(1)}) custom-call(bf16[128,2048]{1,0:T(8,128)(2,1)S(1)} %copy-done.15, bf16[1024,256]{1,0:T(8,128)(2,1)S(1)} %copy-done.10, s32[128,1]{1,0:T(8,128)S(1)} %add.478.qplace_ref, s32[1,1024]{1,0:T(1,128)S(1)} %add.452.kplace_ref, bf16[128,2048]{1,0:T(8,128)(2,1)S(1)} %copy-done.12, ...), custom_call_target="tpu_custom_call" | custom-call | flops 10737418240 | bytes 80000000 | tf_op jit(solution)/shard_map/attend_backward/pallas_call | solution.py:171
  278.7 51.1 %all-to-all-done.3 = bf16[32,24,2048]{2,1,0:T(8,128)(2,1)} async-done(((bf16[32,24,2048]{2,1,0:T(8,128)(2,1)}), bf16[32,24,2048]{2,1,0:T(8,128)(2,1)}, u32[]{:S(2)}, u32[]{:S(2)}) %all-to-all-start.3) | async-done | bytes 3145760 | tf_op jit(solution)/shard_map/all_to_all | solution.py:225
  329.9 4.1 %all-to-all-start.4 = ((bf16[8,128,256]{2,1,0:T(8,128)(2,1)}), bf16[8,128,256]{2,1,0:T(8,128)(2,1)}, u32[]{:S(2)}, u32[]{:S(2)}) async-start(bf16[8,128,256]{2,1,0:T(8,128)(2,1)} %bitcast.89), calls=%async_computation.4 | async-start | bytes 1048576 | tf_op jit(solution)/shard_map/all_to_all | solution.py:374
  334.2 3.6 %fusion.33 = f32[384,2048]{1,0:T(8,128)S(1)} fusion(bf16[768,2048]{1,0:T(8,128)(2,1)} %bitcast.32, bf16[768,128]{1,0:T(8,128)(2,1)S(1)} %broadcast_in_dim.144, bf16[768,128]{1,0:T(8,128)(2,1)} %get-tuple-element.65, bf16[768,128]{1,0:T(8,128)(2,1)S(1)} %get-tuple-element.64), kind=kOutput, calls=%fused_computation.59 | convolution fusion | flops 1209729024 | bytes 6881280 | tf_op jit(solution)/shard_map/dot_general | solution.py:28
  339.4 10.0 %all-to-all-done.4 = bf16[8,128,256]{2,1,0:T(8,128)(2,1)} async-done(((bf16[8,128,256]{2,1,0:T(8,128)(2,1)}), bf16[8,128,256]{2,1,0:T(8,128)(2,1)}, u32[]{:S(2)}, u32[]{:S(2)}) %all-to-all-start.4) | async-done | bytes 524320 | tf_op jit(solution)/shard_map/all_to_all | solution.py:374
  (117 shorter events, 40.6 us)
Async XLA Ops:
  0.6 169.0 %copy-start = (bf16[1,768,2048]{2,1,0:T(8,128)(2,1)S(1)}, bf16[1,768,2048]{2,1,0:T(8,128)(2,1)}, u32[]{:S(2)}) copy-start(bf16[1,768,2048]{2,1,0:T(8,128)(2,1)} %param.22) | copy-start | bytes 9437188
  27.3 5.6 %copy-start.26 = (s32[16]{0:T(128)S(1)}, s32[16]{0:T(128)}, u32[]{:S(2)}) copy-start(s32[16]{0:T(128)} %param.16) | copy-start | bytes 196
  27.3 67.0 %all-to-all-start = ((bf16[32,40,1024]{2,1,0:T(8,128)(2,1)}), bf16[32,40,1024]{2,1,0:T(8,128)(2,1)}, u32[]{:S(2)}, u32[]{:S(2)}) async-start(bf16[32,40,1024]{2,1,0:T(8,128)(2,1)} %bitcast.90), calls=%async_computation | async-start | bytes 5242880 | tf_op jit(solution)/shard_map/all_to_all | solution.py:225
  35.5 12.9 %copy-start.22 = (bf16[128,2048]{1,0:T(8,128)(2,1)S(1)}, bf16[128,2048]{1,0:T(8,128)(2,1)}, u32[]{:S(2)}) copy-start(bf16[128,2048]{1,0:T(8,128)(2,1)} %param.12) | copy-start | bytes 1572868
  35.5 14.8 %copy-start.23 = (f32[2048]{0:T(1024)S(1)}, f32[2048]{0:T(1024)}, u32[]{:S(2)}) copy-start(f32[2048]{0:T(1024)} %param.19) | copy-start | bytes 24580
  94.3 64.9 %all-to-all-start.1 = ((bf16[32,40,1024]{2,1,0:T(8,128)(2,1)}), bf16[32,40,1024]{2,1,0:T(8,128)(2,1)}, u32[]{:S(2)}, u32[]{:S(2)}) async-start(bf16[32,40,1024]{2,1,0:T(8,128)(2,1)} %bitcast.91), calls=%async_computation.1 | async-start | bytes 5242880 | tf_op jit(solution)/shard_map/all_to_all | solution.py:225
  159.2 5.4 %copy-start.24 = (bf16[1,2048,768]{2,1,0:T(8,128)(2,1)S(1)}, bf16[1,2048,768]{2,1,0:T(8,128)(2,1)}, u32[]{:S(2)}) copy-start(bf16[1,2048,768]{2,1,0:T(8,128)(2,1)} %param.20) | copy-start | bytes 9437188
  164.6 2.8 copy-start.25
  173.6 2.2 copy-start.27
  173.6 2.2 copy-start.30
  182.3 64.9 %all-to-all-start.2 = ((bf16[32,40,1024]{2,1,0:T(8,128)(2,1)}), bf16[32,40,1024]{2,1,0:T(8,128)(2,1)}, u32[]{:S(2)}, u32[]{:S(2)}) async-start(bf16[32,40,1024]{2,1,0:T(8,128)(2,1)} %bitcast.88), calls=%async_computation.2 | async-start | bytes 5242880 | tf_op jit(solution)/shard_map/all_to_all | solution.py:225
  189.4 4.3 %copy-start.7 = (bf16[640,2048]{1,0:T(8,128)(2,1)S(1)}, bf16[640,2048]{1,0:T(8,128)(2,1)}, u32[]{:S(2)}) copy-start(bf16[640,2048]{1,0:T(8,128)(2,1)} %copy-done.6) | copy-start | bytes 7864324
  189.5 4.3 %copy-start.28 = (bf16[640,768]{1,0:T(8,128)(2,1)S(1)}, bf16[640,768]{1,0:T(8,128)(2,1)}, u32[]{:S(2)}) copy-start(bf16[640,768]{1,0:T(8,128)(2,1)} %copy-done.27) | copy-start | bytes 2949124
  193.7 4.1 %copy-start.31 = (bf16[640,768]{1,0:T(8,128)(2,1)S(1)}, bf16[640,768]{1,0:T(8,128)(2,1)}, u32[]{:S(2)}) copy-start(bf16[640,768]{1,0:T(8,128)(2,1)} %copy-done.30) | copy-start | bytes 2949124
  197.8 4.1 %copy-start.5 = (bf16[640,2048]{1,0:T(8,128)(2,1)S(1)}, bf16[640,2048]{1,0:T(8,128)(2,1)}, u32[]{:S(2)}) copy-start(bf16[640,2048]{1,0:T(8,128)(2,1)} %copy-done.3) | copy-start | bytes 7864324
  197.8 4.1 %copy-start.29 = (bf16[640,768]{1,0:T(8,128)(2,1)S(1)}, bf16[640,768]{1,0:T(8,128)(2,1)}, u32[]{:S(2)}) copy-start(bf16[640,768]{1,0:T(8,128)(2,1)} %get-tuple-element.53) | copy-start | bytes 2949124
  247.2 3.2 copy-start.19
  253.4 4.7 %copy-start.10 = (bf16[1024,256]{1,0:T(8,128)(2,1)S(1)}, bf16[1024,256]{1,0:T(8,128)(2,1)}, u32[]{:S(2)}) copy-start(bf16[1024,256]{1,0:T(8,128)(2,1)} %all_gather.3.kv_ref) | copy-start | bytes 1572868
  253.4 4.7 %copy-start.15 = (bf16[128,2048]{1,0:T(8,128)(2,1)S(1)}, bf16[128,2048]{1,0:T(8,128)(2,1)}, u32[]{:S(2)}) copy-start(bf16[128,2048]{1,0:T(8,128)(2,1)} %q_ref.3) | copy-start | bytes 1572868
  253.4 4.7 %copy-start.17 = (f32[16,256,1]{2,1,0:T(8,128)S(1)}, f32[16,256,1]{2,1,0:T(8,128)}, u32[]{:S(2)}) copy-start(f32[16,256,1]{2,1,0:T(8,128)} %copy-done.16) | copy-start | bytes 49156
  253.4 76.5 %all-to-all-start.3 = ((bf16[32,24,2048]{2,1,0:T(8,128)(2,1)}), bf16[32,24,2048]{2,1,0:T(8,128)(2,1)}, u32[]{:S(2)}, u32[]{:S(2)}) async-start(bf16[32,24,2048]{2,1,0:T(8,128)(2,1)} %broadcast_dynamic-update-slice_fusion), calls=%async_computation.3 | async-start | bytes 6291456 | tf_op jit(solution)/shard_map/all_to_all | solution.py:225
  329.9 19.5 %all-to-all-start.4 = ((bf16[8,128,256]{2,1,0:T(8,128)(2,1)}), bf16[8,128,256]{2,1,0:T(8,128)(2,1)}, u32[]{:S(2)}, u32[]{:S(2)}) async-start(bf16[8,128,256]{2,1,0:T(8,128)(2,1)} %bitcast.89), calls=%async_computation.4 | async-start | bytes 1048576 | tf_op jit(solution)/shard_map/all_to_all | solution.py:374
  334.2 4.2 %copy-start.20 = (bf16[128,2048]{1,0:T(8,128)(2,1)S(1)}, bf16[128,2048]{1,0:T(8,128)(2,1)}, u32[]{:S(2)}) copy-start(bf16[128,2048]{1,0:T(8,128)(2,1)} %copy-done.18) | copy-start | bytes 1572868
  334.2 16.9 %copy-start.1 = (bf16[1,768,2048]{2,1,0:T(8,128)(2,1)S(1)}, bf16[1,768,2048]{2,1,0:T(8,128)(2,1)}, u32[]{:S(2)}) copy-start(bf16[1,768,2048]{2,1,0:T(8,128)(2,1)} %param.22) | copy-start | bytes 9437188
  (13 other events, 16.5 us)
